TPU v7x, 1024 devices: a whole 8x8x8 slice. The times are simulated.
1024 devices in a mesh: row: 8 (over z), col: 128 (over y, x, core).
Axes of the slice: x: 8, y: 8, z: 8, core: 2. Of those that a mesh axis runs over, the one named last changes fastest.
Arguments:
- coarse_scalar: float32 [512, 1024, 128], P('row', 'col'), may hold values from -6 to 6
- coarse_velocity: float32 [3, 512, 1024, 128], P(None, 'row', 'col'), may hold values from -0.5 to 0.5
- coarse_previous: float32 [3, 512, 1024, 128], P(None, 'row', 'col'), may hold values from -0.5 to 0.5
- fine_scalar: float32 [256, 1024, 128], P('row', 'col'), may hold values from -6 to 6
- fine_velocity: float32 [3, 256, 1024, 128], P(None, 'row', 'col'), may hold values from -0.5 to 0.5
- fine_previous: float32 [3, 256, 1024, 128], P(None, 'row', 'col'), may hold values from -0.5 to 0.5
- parent_shift: int32 [8, 128], P('row'), may hold values from -3 to 3, as said below
- offset_y: int32 [8, 128], P('row'), may hold values from 1 to 3
- offset_z: int32 [8, 128], P('row'), may hold values from 1 to 63
Outputs:
- coarse_result: float32 [512, 1024, 128], P('row', 'col')
- fine_result: float32 [256, 1024, 128], P('row', 'col')
Inputs may be any that keep to these rules, and one draw needn't show every extreme that they name: `parent_shift`: in every aligned block of four columns of a row, every fine box's parent lies in the same block and never in its own column; one coarse box of each block is the parent of three fine boxes, another of one.
All inputs are finite; a program needn't handle non-finite values.
Results may differ from a plain program's by a relative error of at most 0.0003.
Values sent between devices are 32-bit elements; how exact they have to be, the bound alone decides.
A program may use at most 64 MiB of HBM per device.

v0:
```python
import jax
import jax.numpy as jnp
from jax import lax
from jax.experimental import pallas as pl
from jax.experimental.pallas import tpu as pltpu
from jax.sharding import PartitionSpec as P

MESH = pl.DeviceIdType.MESH
F32 = jnp.float32
NX = 64
WX = 22
TILES = 5


def minmod(p, q):
    return jnp.maximum(jnp.minimum(p, q), 0.0) + jnp.minimum(jnp.maximum(p, q), 0.0)


def flux(sl, ml, sr, mr, w):
    q = 0.15 * w
    return w * jnp.where(w > 0, sl + (0.5 - q) * ml, sr - (0.5 + q) * mr)


def split_dot(values, matrix):
    high = values.astype(jnp.bfloat16)
    low = (values - high.astype(F32)).astype(jnp.bfloat16)
    return jnp.dot(high, matrix, preferred_element_type=F32) + jnp.dot(low, matrix, preferred_element_type=F32)


def split_dot_left(matrix, values):
    high = values.astype(jnp.bfloat16)
    low = (values - high.astype(F32)).astype(jnp.bfloat16)
    return jnp.dot(matrix, high, preferred_element_type=F32) + jnp.dot(matrix, low, preferred_element_type=F32)


def tile_iota(dim):
    return lax.broadcasted_iota(jnp.int32, (8, 128), dim)


def y_fluxes(s, b):
    d = [s[i + 1] - s[i] for i in range(4)]
    m = [minmod(d[i], d[i + 1]) for i in range(3)]
    low = flux(s[1], m[0], s[2], m[1], b[0] + b[1])
    high = flux(s[2], m[1], s[3], m[2], b[1] + b[2])
    return low, high


def kernel(
    cs, cv, cp, fs, fv, fp, shift, offy, offz,
    out_c, out_f,
    own, partner, xlow, xhigh, ysend, yrecv, slab, msend, mbuf, base, masks,
    gh, fine, s1, s1z, fxs, ry, rz, wavg, wx, vsend, vrecv,
    send_sem, recv_sem,
):
    rows = lax.axis_size("row")
    cols = lax.axis_size("col")
    r = lax.axis_index("row")
    c = lax.axis_index("col")
    core = lax.rem(c, 2)
    j_me = lax.rem(c, 4)
    g0 = c - j_me
    sgn = 2 * core - 1
    r_up = lax.rem(r + 1, rows)
    r_dn = lax.rem(r + rows - 1, rows)
    mate = c + 1 - 2 * core

    def peer(d):
        bit0, bit1 = lax.rem(j_me, 2), j_me // 2
        if d & 1:
            bit0 = 1 - bit0
        if d & 2:
            bit1 = 1 - bit1
        return g0 + 2 * bit1 + bit0

    near = lax.rem(c + sgn + cols, cols)
    far = lax.rem(c + 2 * sgn + cols, cols)

    barrier = pltpu.get_barrier_semaphore()
    greet = [
        (r, peer(1)), (r, peer(2)), (r, peer(3)),
        (r_up, c), (r_dn, c), (r_up, mate), (r_dn, mate),
        (r, near), (r, lax.rem(c + 2, cols)), (r, lax.rem(c + cols - 2, cols)),
    ]
    for dev in greet:
        pl.semaphore_signal(barrier, inc=1, device_id=dev, device_id_type=MESH)

    row = tile_iota(0)
    lane = tile_iota(1)
    l0 = lane == 0
    l127 = lane == 127

    par = [j + shift[0, g0 + j] for j in range(4)]
    oyv = [offy[0, g0 + j] for j in range(4)]
    ozv = [offz[0, g0 + j] for j in range(4)]
    one = jnp.int32(1)
    zero = jnp.int32(0)
    rank = []
    for j in range(4):
        acc = zero
        for i in range(j):
            acc = acc + jnp.where(par[i] == par[j], one, zero)
        rank.append(acc)

    def pick(values, t):
        acc = zero
        for j in range(4):
            acc = acc + jnp.where(t == j, values[j], zero)
        return acc

    def half_coarse(x, carry):
        own[0, x] = cs[x]
        for f in range(3):
            own[f + 1, x] = 0.75 * cv[f, x] - 0.25 * cp[f, x]
        even = [pltpu.roll(own[f, x], 2 * f, 0) if f else own[f, x] for f in range(4)]
        odd = [pltpu.roll(own[f, x], (2 * f + 2) % 8, 0) if f != 3 else own[f, x] for f in range(4)]
        pe, po = even[0], odd[0]
        for f in range(1, 4):
            here = (row >= 2 * f) & (row < 2 * f + 2)
            pe = jnp.where(here, even[f], pe)
            po = jnp.where(here, odd[f], po)
        ysend[x] = jnp.where(core == 0, pe, po)
        return carry

    lax.fori_loop(0, NX, half_coarse, 0)
    pl.semaphore_wait(barrier, len(greet))

    def copy(src, dst, k, dev, kr=None):
        return pltpu.make_async_remote_copy(
            src_ref=src, dst_ref=dst, send_sem=send_sem.at[k], recv_sem=recv_sem.at[k if kr is None else kr],
            device_id=dev, device_id_type=MESH,
        )

    box_copy = copy(own, partner, 0, (r, mate))
    up_copy = copy(own.at[:, pl.ds(NX - 2, 2)], xlow.at[0], 1, (r_up, c))
    up_mate_copy = copy(own.at[:, pl.ds(NX - 2, 2)], xlow.at[1], 2, (r_up, mate))
    down_copy = copy(own.at[:, pl.ds(0, 2)], xhigh, 3, (r_dn, c))
    near_copy = copy(ysend, yrecv.at[1 - core], 4, (r, near), 5 - core)
    far_copy = copy(ysend, yrecv.at[1 - core], 5, (r, far), 5 - core)
    first_copies = (near_copy, far_copy, box_copy, up_copy, up_mate_copy, down_copy)
    for one_copy in first_copies:
        one_copy.start()

    def half_fine(x, carry):
        fine[0, 0, x + 4, pl.ds(4, 8), :] = fs[x]
        for f in range(3):
            fine[f + 1, 0, x + 4, pl.ds(4, 8), :] = 0.75 * fv[f, x] - 0.25 * fp[f, x]
        return carry

    lax.fori_loop(0, 32, half_fine, 0)

    slots = []
    for k in range(3):
        slot, oyk, ozk, valid = zero, zero, zero, zero
        for j in range(4):
            mine = jnp.where((par[j] == j_me) & (rank[j] == k), one, zero)
            dist0 = jnp.where(lax.rem(j_me, 2) == j % 2, zero, one)
            dist1 = jnp.where(j_me // 2 == j // 2, zero, one)
            slot = slot + mine * (dist0 + 2 * dist1)
            oyk = oyk + mine * oyv[j]
            ozk = ozk + mine * ozv[j]
            valid = valid + mine
        slots.append(slot)
        oyk = jnp.where(valid > 0, oyk, -100)
        iny = (row >= oyk) & (row < oyk + 4)
        inz = (lane >= ozk) & (lane < ozk + 64)
        masks[k, 0] = jnp.where((row == oyk - 1) & inz, 0.3, 0.0)
        masks[k, 1] = jnp.where((row == oyk + 4) & inz, 0.3, 0.0)
        masks[k, 2] = jnp.where((lane == ozk - 1) & iny, 0.3, 0.0)
        masks[k, 3] = jnp.where((lane == ozk + 64) & iny, 0.3, 0.0)
        masks[k, 4] = jnp.where(iny & inz, 1.0, 0.0)
    for q in range(5):
        masks[3, q] = jnp.zeros((8, 128), F32)

    base_row = pl.multiple_of(8 + 8 * core, 8)
    mate_row = pl.multiple_of(16 - 8 * core, 8)
    chip = c // 2
    has_low = chip > 0
    has_high = chip < cols // 2 - 1
    row_low = r > 0
    row_high = r < rows - 1

    for h in range(2):
        copy(ysend, yrecv.at[h], 4 + h, (r, near)).wait_recv()
    for k in (0, 1, 2, 3):
        (box_copy, up_copy, up_mate_copy, down_copy)[k].wait_recv()

    def assemble(x, carry):
        for f in range(4):
            slab[f, x + 2, pl.ds(base_row, 8), :] = own[f, x]
            slab[f, x + 2, pl.ds(mate_row, 8), :] = partner[f, x]
            slab[f, x + 2, pl.ds(6, 2), :] = jnp.where(has_low, yrecv[0, x, pl.ds(2 * f, 2), :], 0.0)
            slab[f, x + 2, pl.ds(24, 2), :] = jnp.where(has_high, yrecv[1, x, pl.ds(2 * f, 2), :], 0.0)
        return carry

    lax.fori_loop(0, NX, assemble, 0)
    for f in range(4):
        for i in range(2):
            slab[f, i, pl.ds(base_row, 8), :] = jnp.where(row_low, xlow[0, f, i], 0.0)
            slab[f, i, pl.ds(mate_row, 8), :] = jnp.where(row_low, xlow[1, f, i], 0.0)
            slab[f, NX + 2 + i, pl.ds(base_row, 8), :] = jnp.where(row_high, xhigh[f, i], 0.0)

    def extract(t, store):
        p = pick(par, t)
        first = 18 * pick(rank, t)
        r0 = 5 + 8 * lax.rem(p, 2) + pick(oyv, t)

        def plane(i, carry):
            x = first + i
            store(TILES * i, slab[0, x, pl.ds(r0 + 1, 8), :])
            store(TILES * i + 1, slab[1, x, pl.ds(r0 + 1, 8), :])
            store(TILES * i + 2, slab[2, x, pl.ds(r0 + 1, 8), :])
            store(TILES * i + 3, slab[3, x, pl.ds(r0 + 1, 8), :])
            edge = slab[0, x, pl.ds(r0, 8), :]
            edge = jnp.where(row == 7, slab[0, x, pl.ds(r0 + 2, 8), :], edge)
            edge = jnp.where(row == 1, slab[2, x, pl.ds(r0 - 1, 8), :], edge)
            edge = jnp.where(row == 6, slab[2, x, pl.ds(r0 + 3, 8), :], edge)
            store(TILES * i + 4, edge)
            return carry

        lax.fori_loop(0, WX, plane, 0)

    def store_send(k, value):
        msend[k] = value

    def store_own(k, value):
        mbuf[0, k] = value

    j_cross = lax.rem(j_me + 2, 4)
    extract(j_cross, store_send)
    patch_copy = copy(msend, mbuf.at[1], 6, (r, peer(2)))
    patch_copy.start()
    extract(j_me, store_own)

    def coarse_load(f, x, delta=0):
        return slab[f, x, pl.ds(base_row + delta, 8), :]

    def coarse_plane(x, carry):
        fxl, mx, sx, sn, ax = carry
        snn = coarse_load(0, x + 4)
        an = coarse_load(1, x + 3)
        mn = minmod(sn - sx, snn - sn)
        fxu = flux(sx, mx, sn, mn, ax + an)
        ys = [coarse_load(0, x + 2, d) for d in (-2, -1, 0, 1, 2)]
        yb = [coarse_load(2, x + 2, d) for d in (-1, 0, 1)]
        fyl, fyu = y_fluxes(ys, yb)
        vz = coarse_load(3, x + 2)
        up = jnp.where(l127, 0.0, pltpu.roll(sx, 127, 1))
        dn = jnp.where(l0, 0.0, pltpu.roll(sx, 1, 1))
        mz = minmod(sx - dn, up - sx)
        mu = jnp.where(l127, 0.0, pltpu.roll(mz, 127, 1))
        vu = jnp.where(l127, 0.0, pltpu.roll(vz, 127, 1))
        fzu = flux(sx, mz, up, mu, vz + vu)
        w0 = jnp.minimum(vz, 0.0)
        fzl = jnp.where(l0, w0 * (sx - (0.5 + 0.15 * w0) * mz), pltpu.roll(fzu, 1, 1))
        new = sx - 0.3 * ((fxu - fxl) + (fyu - fyl) + (fzu - fzl))
        k = x // 18
        i = x - 18 * k
        mid = jnp.where((i >= 1) & (i <= 16), 1.0, 0.0).astype(F32)
        lowx = jnp.where(i == 0, 0.3, 0.0).astype(F32)
        highx = jnp.where(i == 17, 0.3, 0.0).astype(F32)
        cov = masks[k, 4]
        new = new + mid * (masks[k, 0] * fyu - masks[k, 1] * fyl + masks[k, 2] * fzu - masks[k, 3] * fzl)
        new = new + cov * (lowx * fxu - highx * fxl)
        base[x] = jnp.where(cov * mid > 0, 0.0, new)
        return fxu, mn, sn, snn, an

    def coarse_pair(h, carry):
        for e in range(2):
            carry = coarse_plane(2 * h + e, carry)
        return carry

    p0, p1, p2, p3 = [coarse_load(0, i) for i in range(4)]
    v1, v2 = coarse_load(1, 1), coarse_load(1, 2)
    m1, m2 = minmod(p1 - p0, p2 - p1), minmod(p2 - p1, p3 - p2)
    lax.fori_loop(0, NX // 2, coarse_pair, (flux(p1, m1, p2, m2, v1 + v2), m2, p2, p3, v2))

    my_par = pick(par, j_me)
    my_oy = pick(oyv, j_me)
    my_oz = pick(ozv, j_me)
    sel = jnp.where(my_par // 2 == j_me // 2, zero, one)
    zi = lax.broadcasted_iota(jnp.int32, (128, 512), 0)
    qi = lax.broadcasted_iota(jnp.int32, (128, 512), 1)
    lq = qi & 127
    cell0 = my_oz + (lq >> 1)
    cell1 = jnp.where(lq < 4, my_oz + 64 + (lq >> 1), jnp.where(lq >= 124, my_oz + ((lq - 128) >> 1), -1000))
    cell = jnp.where((qi & 128) == 0, cell0, cell1)
    slope = jnp.where(qi >= 256, jnp.where((qi & 1) == 0, -0.125, 0.125), 0.0)
    zmat = jnp.where(zi == cell, 1.0, 0.0) + jnp.where(zi == cell + 1, slope, 0.0) - jnp.where(zi == cell - 1, slope, 0.0)
    zmat = zmat.astype(jnp.bfloat16)

    patch_copy.wait_recv()
    half = WX * TILES // 2
    for h in range(2):
        lhs = mbuf[sel, pl.ds(h * half, half)].reshape(half * 8, 128)
        res = split_dot(lhs, zmat)
        for q in range(4):
            gh[q, pl.ds(h * half, half)] = res[:, 128 * q:128 * (q + 1)].reshape(half, 8, 128)

    def refine_plane(i, full):
        for lt in range(2):
            edge = gh[lt, TILES * i + 4]
            for f in range(4):
                g = gh[lt, TILES * i + f]
                sx = 0.125 * (gh[lt, TILES * (i + 1) + f] - gh[lt, TILES * (i - 1) + f])
                lo = pltpu.roll(g, 1, 0)
                hi = pltpu.roll(g, 7, 0)
                if f == 0:
                    lo = jnp.where(row == 0, edge, lo)
                    hi = jnp.where(row == 7, edge, hi)
                if f == 2:
                    lo = jnp.where(row == 0, pltpu.roll(edge, 7, 0), lo)
                    hi = jnp.where(row == 7, pltpu.roll(edge, 1, 0), hi)
                sy = 0.125 * (hi - lo)
                ctr = gh[2 + lt, TILES * i + f]
                for e in range(2):
                    cx = ctr + sx if e else ctr - sx
                    for ey in range(2):
                        value = cx + sy if ey else cx - sy
                        xf = 2 * (i - 1) + e
                        if full or lt == 1:
                            fine[f, lt, xf, pl.ds(ey, 8, stride=2), :] = value
                        else:
                            fine[f, lt, xf, pl.ds(ey, 2, stride=2), :] = value[0:2]
                            fine[f, lt, xf, pl.ds(12 + ey, 2, stride=2), :] = value[6:8]

    def refine_ends(i, carry):
        refine_plane(jnp.where(i < 2, i + 1, i + 17), True)
        return carry

    def refine_middle(i, carry):
        refine_plane(i, False)
        return carry

    lax.fori_loop(0, 4, refine_ends, 0)
    lax.fori_loop(3, 19, refine_middle, 0)

    def zup(t0, t1):
        a0, a1 = pltpu.roll(t0, 127, 1), pltpu.roll(t1, 127, 1)
        return jnp.where(l127, a1, a0), jnp.where(l127, a0, a1)

    def zdn(t0, t1):
        a0, a1 = pltpu.roll(t0, 1, 1), pltpu.roll(t1, 1, 1)
        return jnp.where(l0, a1, a0), jnp.where(l0, a0, a1)

    def z_fluxes(t0, t1, w0, w1):
        u0, u1 = zup(t0, t1)
        d0, d1 = zdn(t0, t1)
        n0, n1 = minmod(t0 - d0, u0 - t0), minmod(t1 - d1, u1 - t1)
        nu0, nu1 = zup(n0, n1)
        wu0, wu1 = zup(w0, w1)
        h0, h1 = flux(t0, n0, u0, nu0, w0 + wu0), flux(t1, n1, u1, nu1, w1 + wu1)
        b0, b1 = zdn(h0, h1)
        return b0, h0, b1, h1

    def load(block, f, x, d=0):
        if block == 0:
            return fine[f, 0, x, pl.ds(4 + d, 8), :]
        if block == 1:
            return fine[f, 1, x, pl.ds(4 + d, 8), :]
        return jnp.where(row < 4, fine[f, 0, x, pl.ds(2 + d, 8), :], fine[f, 0, x, pl.ds(6 + d, 8), :])

    def load_pad(f, x):
        return jnp.where(row < 4, fine[f, 1, x, pl.ds(2, 8), :], fine[f, 1, x, pl.ds(6, 8), :])

    def x_start(block, x):
        a0, a1, a2, a3 = [load(block, 0, x + d) for d in (-2, -1, 0, 1)]
        w0, w1 = load(block, 1, x - 1), load(block, 1, x)
        n1, n2 = minmod(a1 - a0, a2 - a1), minmod(a2 - a1, a3 - a2)
        return flux(a1, n1, a2, n2, w0 + w1), n2, a2, a3, w1

    def x_next(block, x, carry):
        fxl, mx, sx, sn, ax = carry
        snn = load(block, 0, x + 2)
        an = load(block, 1, x + 1)
        mn = minmod(sn - sx, snn - sn)
        fxu = flux(sx, mx, sn, mn, ax + an)
        return fxl, fxu, (fxu, mn, sn, snn, an)

    def first_plane(x, carries):
        out, xs, ys = [], [], []
        for block in range(3):
            fxl, fxu, nxt = x_next(block, x, carries[block])
            out.append(nxt)
            xs.append((fxl, fxu))
            ys.append(y_fluxes([load(block, 0, x, d) for d in (-2, -1, 0, 1, 2)], [load(block, 2, x, d) for d in (-1, 0, 1)]))
        c0, c1, c2 = carries[0][2], carries[1][2], carries[2][2]
        zl0, zu0, zl1, zu1 = z_fluxes(c0, c1, load(0, 3, x), load(1, 3, x))
        zl2, zu2, _, _ = z_fluxes(c2, load_pad(0, x), load(2, 3, x), load_pad(3, x))
        news = []
        for sc, (xl, xu), (yl, yu), (zl, zu) in zip((c0, c1, c2), xs, ys, ((zl0, zu0), (zl1, zu1), (zl2, zu2))):
            news.append(sc - 0.3 * ((xu - xl) + (yu - yl) + (zu - zl)))
        s1[x - 2, pl.ds(2, 8), :] = news[0]
        s1[x - 2, pl.ds(0, 2), :] = news[2][0:2]
        s1[x - 2, pl.ds(10, 2), :] = news[2][6:8]
        s1z[x - 2] = news[1]
        reg_y = jnp.where(row == 0, ys[0][0], jnp.where(row == 7, ys[0][1], 0.0))
        reg_z = jnp.where(l0, zl0, jnp.where(l127, zu0, 0.0))
        return tuple(out), reg_y, reg_z, xs[0][1]

    def first_pair(h, carries):
        carries, ya, za, _ = first_plane(2 + 2 * h, carries)
        carries, yb, zb, fx = first_plane(3 + 2 * h, carries)
        ry[h] = ya + yb
        rz[h] = za + zb
        fxs[h] = fx
        return carries

    lax.fori_loop(0, 18, first_pair, tuple(x_start(block, 2) for block in range(3)))

    def second_load(x, d=0):
        return s1[x + 2, pl.ds(2 + d, 8), :]

    def second_plane(x, carry):
        fxl, mx, sx, sn, ax = carry
        snn = second_load(x + 2)
        an = load(0, 1, x + 5)
        mn = minmod(sn - sx, snn - sn)
        fxu = flux(sx, mx, sn, mn, ax + an)
        yl, yu = y_fluxes([second_load(x, d) for d in (-2, -1, 0, 1, 2)], [load(0, 2, x + 4, d) for d in (-1, 0, 1)])
        zl, zu, _, _ = z_fluxes(sx, s1z[x + 2], load(0, 3, x + 4), load(1, 3, x + 4))
        new = sx - 0.3 * ((fxu - fxl) + (yu - yl) + (zu - zl))
        out_f[x] = new
        reg_y = jnp.where(row == 0, yl, jnp.where(row == 7, yu, 0.0))
        reg_z = jnp.where(l0, zl, jnp.where(l127, zu, 0.0))
        return (fxu, mn, sn, snn, an), new, reg_y, reg_z

    def second_pair(h, carry):
        carry, na, ya, za = second_plane(2 * h, carry)
        carry, nb, yb, zb = second_plane(2 * h + 1, carry)
        at = pl.ds(pl.multiple_of(8 * h, 8), 8)
        wavg[0, at, :] = 0.125 * (na + nb)
        wavg[1, at, :] = 0.0375 * (rz[h + 1] + (za + zb))
        wavg[2, at, :] = 0.0375 * (ry[h + 1] + (ya + yb))
        return carry

    q0, q1, q2, q3 = [second_load(i) for i in (-2, -1, 0, 1)]
    u1, u2 = load(0, 1, 3), load(0, 1, 4)
    k1, k2 = minmod(q1 - q0, q2 - q1), minmod(q2 - q1, q3 - q2)
    x_low = flux(q1, k1, q2, k2, u1 + u2)
    x_high = lax.fori_loop(0, 16, second_pair, (x_low, k2, q2, q3, u2))[0]
    wx[...] = jnp.zeros((128, 128), F32)
    wx[pl.ds(0, 8), :] = -0.0375 * (fxs[0] + x_low)
    wx[pl.ds(8, 8), :] = 0.0375 * (fxs[16] + x_high)

    ri = lax.broadcasted_iota(jnp.int32, (128, 128), 0)
    ci = lax.broadcasted_iota(jnp.int32, (128, 128), 1)
    to_z = jnp.where(ci == my_oz + (ri >> 1), 1.0, 0.0).astype(jnp.bfloat16)
    to_zface = jnp.where((ri == 127) & (ci == my_oz + 64), 1.0, 0.0) - jnp.where((ri == 0) & (ci == my_oz - 1), 1.0, 0.0)
    to_zface = to_zface.astype(jnp.bfloat16)
    same = (ri >> 3) == (ci >> 3)
    yr, yc = ri & 7, ci & 7
    to_y = jnp.where(same & (yr == my_oy + (yc >> 1)), 1.0, 0.0).astype(jnp.bfloat16)
    to_yface = jnp.where(same & (yc == 7) & (yr == my_oy + 4), 1.0, 0.0) - jnp.where(same & (yc == 0) & (yr == my_oy - 1), 1.0, 0.0)
    to_yface = to_yface.astype(jnp.bfloat16)
    placed = split_dot(wavg[0], to_z) + split_dot(wavg[1], to_zface)
    faces = split_dot(wavg[2], to_z)
    ends = split_dot(wx[...], to_z)
    middle = split_dot_left(to_y, placed) + split_dot_left(to_yface, faces)
    ends = split_dot_left(to_y, ends)
    vsend[pl.ds(1, 16)] = middle.reshape(16, 8, 128)
    vsend[0] = ends[0:8]
    vsend[17] = ends[8:16]

    back = [copy(vsend, vrecv.at[d], 6 + d, (r, peer(d))) for d in (1, 2, 3)]
    for one_copy in back:
        one_copy.start()
    vrecv[0] = jnp.zeros((18, 8, 128), F32)

    def tail(x, carry):
        out_c[x] = base[x]
        return carry

    lax.fori_loop(54, NX, tail, 0)
    for one_copy in back:
        one_copy.wait_recv()
    for k in range(3):
        def finish(i, carry, k=k):
            out_c[18 * k + i] = base[18 * k + i] + vrecv[slots[k], i]
            return carry

        lax.fori_loop(0, 18, finish, 0)
    for one_copy in first_copies + (patch_copy,) + tuple(back):
        one_copy.wait_send()


def per_device(*args):
    vmem = pl.BlockSpec(memory_space=pltpu.VMEM)
    smem = pl.BlockSpec(memory_space=pltpu.SMEM)

    def buf(*shape):
        return pltpu.VMEM(shape + (8, 128), F32)

    return pl.pallas_call(
        kernel,
        out_shape=(
            jax.ShapeDtypeStruct((64, 8, 128), F32),
            jax.ShapeDtypeStruct((32, 8, 128), F32),
        ),
        in_specs=[vmem] * 6 + [smem] * 3,
        out_specs=(vmem, vmem),
        scratch_shapes=[
            buf(4, NX),
            buf(4, NX),
            buf(2, 4, 2),
            buf(4, 2),
            buf(NX),
            buf(2, NX),
            pltpu.VMEM((4, NX + 4, 32, 128), F32),
            buf(WX * TILES),
            buf(2, WX * TILES),
            buf(NX),
            buf(4, 5),
            buf(4, WX * TILES),
            pltpu.VMEM((4, 2, 40, 16, 128), F32),
            pltpu.VMEM((36, 16, 128), F32),
            buf(36),
            buf(18),
            buf(18),
            buf(18),
            pltpu.VMEM((3, 128, 128), F32),
            pltpu.VMEM((128, 128), F32),
            buf(18),
            buf(4, 18),
            pltpu.SemaphoreType.DMA((10,)),
            pltpu.SemaphoreType.DMA((10,)),
        ],
        compiler_params=pltpu.CompilerParams(
            collective_id=0, has_side_effects=True, vmem_limit_bytes=48 * 1024 * 1024
        ),
    )(*args)


def solution(mesh):
    in_specs = (
        P("row", "col", None),
        P(None, "row", "col", None),
        P(None, "row", "col", None),
        P("row", "col", None),
        P(None, "row", "col", None),
        P(None, "row", "col", None),
        P("row", None),
        P("row", None),
        P("row", None),
    )
    out_specs = (P("row", "col", None), P("row", "col", None))
    return jax.shard_map(
        per_device, mesh=mesh, in_specs=in_specs, out_specs=out_specs, check_vma=False
    )
```

profile of v0, /device:TPU:1, one launch (start us, length us, event | category | flops | bytes accessed | tf_op | source)
XLA Modules:
  0.0 64.1 jit_solution(4639833738652388663)
XLA Ops:
  0.6 0.0 copy-start
  0.6 1.1 %copy-done = f32[3,64,8,128]{3,2,1,0:T(8,128)S(1)} copy-done((f32[3,64,8,128]{3,2,1,0:T(8,128)S(1)}, f32[3,64,8,128]{3,2,1,0:T(8,128)}, u32[]{:S(2)}) %copy-start) | copy-done | bytes 786456
  1.8 0.0 copy-start.1
  1.8 1.1 %copy-done.1 = f32[3,64,8,128]{3,2,1,0:T(8,128)S(1)} copy-done((f32[3,64,8,128]{3,2,1,0:T(8,128)S(1)}, f32[3,64,8,128]{3,2,1,0:T(8,128)}, u32[]{:S(2)}) %copy-start.1) | copy-done | bytes 786456
  2.9 0.0 copy-start.2
  2.9 1.0 %copy-done.2 = f32[3,32,8,128]{3,2,1,0:T(8,128)S(1)} copy-done((f32[3,32,8,128]{3,2,1,0:T(8,128)S(1)}, f32[3,32,8,128]{3,2,1,0:T(8,128)}, u32[]{:S(2)}) %copy-start.2) | copy-done | bytes 393240
  3.9 0.0 copy-start.3
  3.9 1.0 %copy-done.3 = f32[3,32,8,128]{3,2,1,0:T(8,128)S(1)} copy-done((f32[3,32,8,128]{3,2,1,0:T(8,128)S(1)}, f32[3,32,8,128]{3,2,1,0:T(8,128)}, u32[]{:S(2)}) %copy-start.3) | copy-done | bytes 393240
  4.9 0.0 copy-start.4
  4.9 0.9 %copy-done.4 = f32[64,8,128]{2,1,0:T(8,128)S(1)} copy-done((f32[64,8,128]{2,1,0:T(8,128)S(1)}, f32[64,8,128]{2,1,0:T(8,128)}, u32[]{:S(2)}) %copy-start.4) | copy-done | bytes 262168
  5.8 0.0 copy-start.5
  5.8 0.9 %copy-done.5 = f32[32,8,128]{2,1,0:T(8,128)S(1)} copy-done((f32[32,8,128]{2,1,0:T(8,128)S(1)}, f32[32,8,128]{2,1,0:T(8,128)}, u32[]{:S(2)}) %copy-start.5) | copy-done | bytes 131096
  6.7 0.0 copy-start.6
  6.8 0.7 %copy-done.6 = s32[1,128]{1,0:T(1,128)S(1)} copy-done((s32[1,128]{1,0:T(1,128)S(1)}, s32[1,128]{1,0:T(1,128)}, u32[]{:S(2)}) %copy-start.6) | copy-done | bytes 536
  7.4 0.0 copy-start.7
  7.4 0.7 %copy-done.7 = s32[1,128]{1,0:T(1,128)S(1)} copy-done((s32[1,128]{1,0:T(1,128)S(1)}, s32[1,128]{1,0:T(1,128)}, u32[]{:S(2)}) %copy-start.7) | copy-done | bytes 536
  8.1 0.0 copy-start.8
  8.1 0.7 %copy-done.8 = s32[1,128]{1,0:T(1,128)S(1)} copy-done((s32[1,128]{1,0:T(1,128)S(1)}, s32[1,128]{1,0:T(1,128)}, u32[]{:S(2)}) %copy-start.8) | copy-done | bytes 536
  8.7 54.1 %shard_map.104 = (f32[64,8,128]{2,1,0:T(8,128)S(1)}, f32[32,8,128]{2,1,0:T(8,128)S(1)}) custom-call(f32[64,8,128]{2,1,0:T(8,128)S(1)} %copy-done.4, f32[3,64,8,128]{3,2,1,0:T(8,128)S(1)} %copy-done, f32[3,64,8,128]{3,2,1,0:T(8,128)S(1)} %copy-done.1, f32[32,8,128]{2,1,0:T(8,128)S(1)} %copy-done.5, f32[3,32,8,128]{3,2,1,0:T(8,128)S(1)} %copy-done.2, ...), custom_call_target="tpu_custom_call" | custom-call | tf_op jit(solution)/shard_map/pallas_call | solution.py:493
  62.8 0.7 %copy.13 = f32[64,8,128]{2,1,0:T(8,128)} copy(f32[64,8,128]{2,1,0:T(8,128)S(1)} %get-tuple-element.4) | data formatting | bytes 524288
  63.5 0.7 %copy.14 = f32[32,8,128]{2,1,0:T(8,128)} copy(f32[32,8,128]{2,1,0:T(8,128)S(1)} %get-tuple-element.5) | data formatting | bytes 262144
Async XLA Ops:
  0.6 1.1 %copy-start = (f32[3,64,8,128]{3,2,1,0:T(8,128)S(1)}, f32[3,64,8,128]{3,2,1,0:T(8,128)}, u32[]{:S(2)}) copy-start(f32[3,64,8,128]{3,2,1,0:T(8,128)} %cv.1) | copy-start | bytes 2359300
  1.8 1.1 %copy-start.1 = (f32[3,64,8,128]{3,2,1,0:T(8,128)S(1)}, f32[3,64,8,128]{3,2,1,0:T(8,128)}, u32[]{:S(2)}) copy-start(f32[3,64,8,128]{3,2,1,0:T(8,128)} %cp.1) | copy-start | bytes 2359300
  2.9 1.0 %copy-start.2 = (f32[3,32,8,128]{3,2,1,0:T(8,128)S(1)}, f32[3,32,8,128]{3,2,1,0:T(8,128)}, u32[]{:S(2)}) copy-start(f32[3,32,8,128]{3,2,1,0:T(8,128)} %fv.1) | copy-start | bytes 1179652
  3.9 1.0 %copy-start.3 = (f32[3,32,8,128]{3,2,1,0:T(8,128)S(1)}, f32[3,32,8,128]{3,2,1,0:T(8,128)}, u32[]{:S(2)}) copy-start(f32[3,32,8,128]{3,2,1,0:T(8,128)} %fp.1) | copy-start | bytes 1179652
  4.9 0.9 %copy-start.4 = (f32[64,8,128]{2,1,0:T(8,128)S(1)}, f32[64,8,128]{2,1,0:T(8,128)}, u32[]{:S(2)}) copy-start(f32[64,8,128]{2,1,0:T(8,128)} %cs.1) | copy-start | bytes 786436
  5.8 0.9 %copy-start.5 = (f32[32,8,128]{2,1,0:T(8,128)S(1)}, f32[32,8,128]{2,1,0:T(8,128)}, u32[]{:S(2)}) copy-start(f32[32,8,128]{2,1,0:T(8,128)} %fs.1) | copy-start | bytes 393220
  6.7 0.7 %copy-start.6 = (s32[1,128]{1,0:T(1,128)S(1)}, s32[1,128]{1,0:T(1,128)}, u32[]{:S(2)}) copy-start(s32[1,128]{1,0:T(1,128)} %shift.1) | copy-start | bytes 1540
  7.4 0.7 %copy-start.7 = (s32[1,128]{1,0:T(1,128)S(1)}, s32[1,128]{1,0:T(1,128)}, u32[]{:S(2)}) copy-start(s32[1,128]{1,0:T(1,128)} %offy.1) | copy-start | bytes 1540
  8.1 0.7 %copy-start.8 = (s32[1,128]{1,0:T(1,128)S(1)}, s32[1,128]{1,0:T(1,128)}, u32[]{:S(2)}) copy-start(s32[1,128]{1,0:T(1,128)} %offz.1) | copy-start | bytes 1540
where the time goes:
time: 64.5 us; the launch traced here: 64.1 us
  Pallas kernels  54.1 us (84%)
  local copies, waits for them, and re-layouts  9.43 us (15%)
  between operations  0.66 us (1%)
    pallas_call x1, Pallas kernels, per_device(): pl.pallas_call(kernel, out_shape=(jax.ShapeDtypeStruct((64, 8, 128), F32)...  54.1 us
    unnamed x20, local copies, waits for them, and re-layouts  9.43 us

commit v1 on v0

--- a/solution.py
+++ b/solution.py
@@ -10,6 +10,7 @@
 NX = 64
 WX = 22
 TILES = 5
+PACK = 3
 
 
 def minmod(p, q):
@@ -46,11 +47,12 @@
 
 
 def kernel(
+    cs_h, cv_h, cp_h, fs_h, fv_h, fp_h, shift_h, offy_h, offz_h,
+    out_c, out_f,
     cs, cv, cp, fs, fv, fp, shift, offy, offz,
-    out_c, out_f,
-    own, partner, xlow, xhigh, ysend, yrecv, slab, msend, mbuf, base, masks,
+    own, partner, xlow, xhigh, ysend, yrecv, slab, msend, mbuf, wide, base, masks,
     gh, fine, s1, s1z, fxs, ry, rz, wavg, wx, vsend, vrecv,
-    send_sem, recv_sem,
+    load_sem, send_sem, recv_sem, ready,
 ):
     rows = lax.axis_size("row")
     cols = lax.axis_size("col")
@@ -60,9 +62,24 @@
     j_me = lax.rem(c, 4)
     g0 = c - j_me
     sgn = 2 * core - 1
-    r_up = lax.rem(r + 1, rows)
-    r_dn = lax.rem(r + rows - 1, rows)
     mate = c + 1 - 2 * core
+    chip = c // 2
+    has_low = chip > 0
+    has_high = chip < cols // 2 - 1
+    row_low = r > 0
+    row_high = r < rows - 1
+    has_side = jnp.where(core == 0, has_low, has_high)
+    out_dir = jnp.where(j_me < 2, -1, 1)
+    has_out = jnp.where(j_me < 2, has_low, has_high)
+    outer = (j_me == 0) | (j_me == 3)
+
+    loads = [pltpu.make_async_copy(src, dst, load_sem.at[k]) for k, (src, dst) in enumerate(
+        [(shift_h, shift), (offy_h, offy), (offz_h, offz), (cs_h, cs)]
+        + [(cv_h.at[f], cv.at[f]) for f in range(3)] + [(cp_h.at[f], cp.at[f]) for f in range(3)]
+        + [(fs_h, fs)] + [(fv_h.at[f], fv.at[f]) for f in range(3)] + [(fp_h.at[f], fp.at[f]) for f in range(3)]
+    )]
+    for load_copy in loads:
+        load_copy.start()
 
     def peer(d):
         bit0, bit1 = lax.rem(j_me, 2), j_me // 2
@@ -72,23 +89,37 @@
             bit1 = 1 - bit1
         return g0 + 2 * bit1 + bit0
 
-    near = lax.rem(c + sgn + cols, cols)
-    far = lax.rem(c + 2 * sgn + cols, cols)
+    near = c + sgn
+    far = c + 2 * sgn
 
     barrier = pltpu.get_barrier_semaphore()
-    greet = [
-        (r, peer(1)), (r, peer(2)), (r, peer(3)),
-        (r_up, c), (r_dn, c), (r_up, mate), (r_dn, mate),
-        (r, near), (r, lax.rem(c + 2, cols)), (r, lax.rem(c + cols - 2, cols)),
-    ]
-    for dev in greet:
+
+    def greet(*dev):
         pl.semaphore_signal(barrier, inc=1, device_id=dev, device_id_type=MESH)
+
+    for d in (1, 2, 3):
+        greet(r, peer(d))
+
+    @pl.when(has_out)
+    def _():
+        greet(r, c + 2 * out_dir)
+
+    @pl.when(has_out & outer)
+    def _():
+        greet(r, c + out_dir)
+
+    @pl.when(row_high)
+    def _():
+        greet(r + 1, c)
+        greet(r + 1, mate)
 
     row = tile_iota(0)
     lane = tile_iota(1)
     l0 = lane == 0
     l127 = lane == 127
 
+    for k in range(3):
+        loads[k].wait()
     par = [j + shift[0, g0 + j] for j in range(4)]
     oyv = [offy[0, g0 + j] for j in range(4)]
     ozv = [offz[0, g0 + j] for j in range(4)]
@@ -107,22 +138,37 @@
             acc = acc + jnp.where(t == j, values[j], zero)
         return acc
 
-    def half_coarse(x, carry):
-        own[0, x] = cs[x]
-        for f in range(3):
-            own[f + 1, x] = 0.75 * cv[f, x] - 0.25 * cp[f, x]
-        even = [pltpu.roll(own[f, x], 2 * f, 0) if f else own[f, x] for f in range(4)]
-        odd = [pltpu.roll(own[f, x], (2 * f + 2) % 8, 0) if f != 3 else own[f, x] for f in range(4)]
-        pe, po = even[0], odd[0]
-        for f in range(1, 4):
-            here = (row >= 2 * f) & (row < 2 * f + 2)
-            pe = jnp.where(here, even[f], pe)
-            po = jnp.where(here, odd[f], po)
-        ysend[x] = jnp.where(core == 0, pe, po)
-        return carry
-
-    lax.fori_loop(0, NX, half_coarse, 0)
-    pl.semaphore_wait(barrier, len(greet))
+    def half_plane(x):
+        values = [cs[x]] + [0.75 * cv[f, x] - 0.25 * cp[f, x] for f in range(3)]
+        for f in range(4):
+            own[f, x] = values[f]
+        return values
+
+    def rows_at(value, at):
+        return jnp.where(core == 0, pltpu.roll(value, at, 0) if at else value, pltpu.roll(value, (at + 2) % 8, 0))
+
+    def half_coarse(h, carry):
+        planes = [half_plane(4 * h + e) for e in range(4)]
+        for t in range(2):
+            tile = rows_at(planes[2 * t][0], 0)
+            for k, value in ((2, planes[2 * t][2]), (4, planes[2 * t + 1][0]), (6, planes[2 * t + 1][2])):
+                tile = jnp.where(row >= k, rows_at(value, k), tile)
+            ysend[3 * h + t] = tile
+        tile = None
+        for e in range(4):
+            for q in range(2):
+                value, at = planes[e][2 * q + 1], 2 * e + q
+                moved = jnp.where(core == 0, pltpu.roll(value, at, 0) if at else value, pltpu.roll(value, (at + 1) % 8, 0))
+                tile = moved if tile is None else jnp.where(row >= at, moved, tile)
+        ysend[3 * h + 2] = tile
+        return carry
+
+    for k in range(3, 10):
+        loads[k].wait()
+    lax.fori_loop(0, NX // 4, half_coarse, 0)
+
+    greeters = 3 + jnp.where(has_out, jnp.where(outer, 2, 1), 0) + jnp.where(row_low, 2, 0)
+    pl.semaphore_wait(barrier, greeters)
 
     def copy(src, dst, k, dev, kr=None):
         return pltpu.make_async_remote_copy(
@@ -131,14 +177,24 @@
         )
 
     box_copy = copy(own, partner, 0, (r, mate))
-    up_copy = copy(own.at[:, pl.ds(NX - 2, 2)], xlow.at[0], 1, (r_up, c))
-    up_mate_copy = copy(own.at[:, pl.ds(NX - 2, 2)], xlow.at[1], 2, (r_up, mate))
-    down_copy = copy(own.at[:, pl.ds(0, 2)], xhigh, 3, (r_dn, c))
+    up_copy = copy(own.at[:, pl.ds(NX - 2, 2)], xlow.at[0], 1, (r + 1, c))
+    up_mate_copy = copy(own.at[:, pl.ds(NX - 2, 2)], xlow.at[1], 2, (r + 1, mate))
+    down_copy = copy(own.at[pl.ds(0, 2), pl.ds(0, 2)], xhigh, 3, (r - 1, c))
     near_copy = copy(ysend, yrecv.at[1 - core], 4, (r, near), 5 - core)
     far_copy = copy(ysend, yrecv.at[1 - core], 5, (r, far), 5 - core)
-    first_copies = (near_copy, far_copy, box_copy, up_copy, up_mate_copy, down_copy)
-    for one_copy in first_copies:
-        one_copy.start()
+
+    @pl.when(has_side)
+    def _():
+        near_copy.start()
+        far_copy.start()
+
+    box_copy.start()
+
+    @pl.when(row_low)
+    def _():
+        pl.semaphore_signal(ready, inc=1, device_id=(r - 1, c), device_id_type=MESH)
+        pl.semaphore_signal(ready, inc=1, device_id=(r - 1, mate), device_id_type=MESH)
+        down_copy.start()
 
     def half_fine(x, carry):
         fine[0, 0, x + 4, pl.ds(4, 8), :] = fs[x]
@@ -146,7 +202,9 @@
             fine[f + 1, 0, x + 4, pl.ds(4, 8), :] = 0.75 * fv[f, x] - 0.25 * fp[f, x]
         return carry
 
-    lax.fori_loop(0, 32, half_fine, 0)
+    for k in range(10, 17):
+        loads[k].wait()
+    lax.fori_loop(0, 32, half_fine, 0, unroll=4)
 
     slots = []
     for k in range(3):
@@ -173,51 +231,65 @@
 
     base_row = pl.multiple_of(8 + 8 * core, 8)
     mate_row = pl.multiple_of(16 - 8 * core, 8)
-    chip = c // 2
-    has_low = chip > 0
-    has_high = chip < cols // 2 - 1
-    row_low = r > 0
-    row_high = r < rows - 1
-
-    for h in range(2):
-        copy(ysend, yrecv.at[h], 4 + h, (r, near)).wait_recv()
-    for k in (0, 1, 2, 3):
-        (box_copy, up_copy, up_mate_copy, down_copy)[k].wait_recv()
-
-    def assemble(x, carry):
-        for f in range(4):
-            slab[f, x + 2, pl.ds(base_row, 8), :] = own[f, x]
-            slab[f, x + 2, pl.ds(mate_row, 8), :] = partner[f, x]
-            slab[f, x + 2, pl.ds(6, 2), :] = jnp.where(has_low, yrecv[0, x, pl.ds(2 * f, 2), :], 0.0)
-            slab[f, x + 2, pl.ds(24, 2), :] = jnp.where(has_high, yrecv[1, x, pl.ds(2 * f, 2), :], 0.0)
-        return carry
-
-    lax.fori_loop(0, NX, assemble, 0)
-    for f in range(4):
-        for i in range(2):
-            slab[f, i, pl.ds(base_row, 8), :] = jnp.where(row_low, xlow[0, f, i], 0.0)
-            slab[f, i, pl.ds(mate_row, 8), :] = jnp.where(row_low, xlow[1, f, i], 0.0)
-            slab[f, NX + 2 + i, pl.ds(base_row, 8), :] = jnp.where(row_high, xhigh[f, i], 0.0)
-
-    def extract(t, store):
+
+    @pl.when(has_low)
+    def _():
+        copy(ysend, yrecv.at[0], 4, (r, mate)).wait_recv()
+
+    @pl.when(has_high)
+    def _():
+        copy(ysend, yrecv.at[1], 5, (r, mate)).wait_recv()
+
+    for side, has in ((0, has_low), (1, has_high)):
+        @pl.when(jnp.logical_not(has))
+        def _(side=side):
+            yrecv[side] = jnp.zeros((3 * NX // 4, 8, 128), F32)
+
+    box_copy.wait_recv()
+
+    def assemble(h, carry):
+        for e in range(4):
+            x = 4 * h + e
+            for f in range(4):
+                slab[f, x + 2, pl.ds(base_row, 8), :] = own[f, x]
+                slab[f, x + 2, pl.ds(mate_row, 8), :] = partner[f, x]
+            for side, at in ((0, 6), (1, 24)):
+                pair = 3 * h + e // 2
+                slab[0, x + 2, pl.ds(at, 2), :] = yrecv[side, pair, pl.ds(4 * (e % 2), 2), :]
+                slab[2, x + 2, pl.ds(at, 2), :] = yrecv[side, pair, pl.ds(4 * (e % 2) + 2, 2), :]
+                alone = 7 if side == 0 else 24
+                slab[1, x + 2, pl.ds(alone, 1), :] = yrecv[side, 3 * h + 2, pl.ds(2 * e, 1), :]
+                slab[3, x + 2, pl.ds(alone, 1), :] = yrecv[side, 3 * h + 2, pl.ds(2 * e + 1, 1), :]
+        return carry
+
+    lax.fori_loop(0, NX // 4, assemble, 0)
+
+    def extractor(t, store):
         p = pick(par, t)
         first = 18 * pick(rank, t)
         r0 = 5 + 8 * lax.rem(p, 2) + pick(oyv, t)
+        turn = 131 - pick(ozv, t)
 
         def plane(i, carry):
             x = first + i
-            store(TILES * i, slab[0, x, pl.ds(r0 + 1, 8), :])
-            store(TILES * i + 1, slab[1, x, pl.ds(r0 + 1, 8), :])
-            store(TILES * i + 2, slab[2, x, pl.ds(r0 + 1, 8), :])
-            store(TILES * i + 3, slab[3, x, pl.ds(r0 + 1, 8), :])
+
+            def rolled(value, to):
+                return pltpu.roll(value, lax.rem(turn + to, 128), 1)
+
+            four = [slab[f, x, pl.ds(r0 + 1, 8), :] for f in range(4)]
             edge = slab[0, x, pl.ds(r0, 8), :]
             edge = jnp.where(row == 7, slab[0, x, pl.ds(r0 + 2, 8), :], edge)
             edge = jnp.where(row == 1, slab[2, x, pl.ds(r0 - 1, 8), :], edge)
             edge = jnp.where(row == 6, slab[2, x, pl.ds(r0 + 3, 8), :], edge)
-            store(TILES * i + 4, edge)
+            rest = rolled(edge, 0)
+            for f in range(4):
+                rest = jnp.where(lane >= 96 + 8 * f, rolled(four[f], 32 + 8 * f), rest)
+            store(PACK * i, jnp.where(lane < 64, rolled(four[0], 0), rolled(four[1], 64)))
+            store(PACK * i + 1, jnp.where(lane < 64, rolled(four[2], 0), rolled(four[3], 64)))
+            store(PACK * i + 2, rest)
             return carry
 
-        lax.fori_loop(0, WX, plane, 0)
+        return plane
 
     def store_send(k, value):
         msend[k] = value
@@ -225,11 +297,43 @@
     def store_own(k, value):
         mbuf[0, k] = value
 
-    j_cross = lax.rem(j_me + 2, 4)
-    extract(j_cross, store_send)
-    patch_copy = copy(msend, mbuf.at[1], 6, (r, peer(2)))
+    cut = 2 * PACK
+    size = (WX - 2) * PACK
+    cross = extractor(lax.rem(j_me + 2, 4), store_send)
+    lax.fori_loop(2, WX, cross, 0, unroll=4)
+    patch_copy = copy(msend.at[pl.ds(cut, size)], mbuf.at[1, pl.ds(cut, size)], 6, (r, peer(2)))
     patch_copy.start()
-    extract(j_me, store_own)
+
+    @pl.when(row_high)
+    def _():
+        pl.semaphore_wait(ready, 2)
+        up_copy.start()
+        up_mate_copy.start()
+
+    mine = extractor(j_me, store_own)
+    lax.fori_loop(2, WX, mine, 0, unroll=4)
+
+    @pl.when(row_low)
+    def _():
+        up_copy.wait_recv()
+        up_mate_copy.wait_recv()
+        for f in range(4):
+            for i in range(2):
+                slab[f, i, pl.ds(base_row, 8), :] = xlow[0, f, i]
+                slab[f, i, pl.ds(mate_row, 8), :] = xlow[1, f, i]
+
+    @pl.when(jnp.logical_not(row_low))
+    def _():
+        for f in range(4):
+            for i in range(2):
+                slab[f, i] = jnp.zeros((32, 128), F32)
+
+    for i in range(2):
+        cross(i, 0)
+    start_copy = copy(msend.at[pl.ds(0, cut)], mbuf.at[1, pl.ds(0, cut)], 10, (r, peer(2)))
+    start_copy.start()
+    for i in range(2):
+        mine(i, 0)
 
     def coarse_load(f, x, delta=0):
         return slab[f, x, pl.ds(base_row + delta, 8), :]
@@ -264,15 +368,20 @@
         base[x] = jnp.where(cov * mid > 0, 0.0, new)
         return fxu, mn, sn, snn, an
 
-    def coarse_pair(h, carry):
-        for e in range(2):
-            carry = coarse_plane(2 * h + e, carry)
-        return carry
-
-    p0, p1, p2, p3 = [coarse_load(0, i) for i in range(4)]
-    v1, v2 = coarse_load(1, 1), coarse_load(1, 2)
-    m1, m2 = minmod(p1 - p0, p2 - p1), minmod(p2 - p1, p3 - p2)
-    lax.fori_loop(0, NX // 2, coarse_pair, (flux(p1, m1, p2, m2, v1 + v2), m2, p2, p3, v2))
+    def coarse_group(h, carry):
+        for e in range(6):
+            carry = coarse_plane(6 * h + e, carry)
+        return carry
+
+    def coarse_start(x):
+        p0, p1, p2, p3 = [coarse_load(0, x + i) for i in range(4)]
+        v1, v2 = coarse_load(1, x + 1), coarse_load(1, x + 2)
+        m1, m2 = minmod(p1 - p0, p2 - p1), minmod(p2 - p1, p3 - p2)
+        return flux(p1, m1, p2, m2, v1 + v2), m2, p2, p3, v2
+
+    coarse_carry = lax.fori_loop(0, 10, coarse_group, coarse_start(0))
+    for x in (60, 61):
+        coarse_carry = coarse_plane(jnp.int32(x), coarse_carry)
 
     my_par = pick(par, j_me)
     my_oy = pick(oyv, j_me)
@@ -285,13 +394,24 @@
     cell1 = jnp.where(lq < 4, my_oz + 64 + (lq >> 1), jnp.where(lq >= 124, my_oz + ((lq - 128) >> 1), -1000))
     cell = jnp.where((qi & 128) == 0, cell0, cell1)
     slope = jnp.where(qi >= 256, jnp.where((qi & 1) == 0, -0.125, 0.125), 0.0)
+    zi = jnp.where((zi < 70) & (zi + my_oz >= 3) & (zi + my_oz < 131), zi + my_oz - 3, -5000)
     zmat = jnp.where(zi == cell, 1.0, 0.0) + jnp.where(zi == cell + 1, slope, 0.0) - jnp.where(zi == cell - 1, slope, 0.0)
     zmat = zmat.astype(jnp.bfloat16)
 
     patch_copy.wait_recv()
+    start_copy.wait_recv()
+
+    def unpack(i, carry):
+        first, second, rest = [mbuf[sel, PACK * i + q] for q in range(PACK)]
+        for f, value in enumerate((first, pltpu.roll(first, 64, 1), second, pltpu.roll(second, 64, 1))):
+            wide[TILES * i + f] = jnp.where(lane < 64, value, pltpu.roll(rest, 96 - 8 * f, 1))
+        wide[TILES * i + 4] = rest
+        return carry
+
+    lax.fori_loop(0, WX, unpack, 0, unroll=2)
     half = WX * TILES // 2
     for h in range(2):
-        lhs = mbuf[sel, pl.ds(h * half, half)].reshape(half * 8, 128)
+        lhs = wide[pl.ds(h * half, half)].reshape(half * 8, 128)
         res = split_dot(lhs, zmat)
         for q in range(4):
             gh[q, pl.ds(h * half, half)] = res[:, 128 * q:128 * (q + 1)].reshape(half, 8, 128)
@@ -405,7 +525,12 @@
         fxs[h] = fx
         return carries
 
-    lax.fori_loop(0, 18, first_pair, tuple(x_start(block, 2) for block in range(3)))
+    def first_group(h, carries):
+        for e in range(3):
+            carries = first_pair(3 * h + e, carries)
+        return carries
+
+    lax.fori_loop(0, 6, first_group, tuple(x_start(block, 2) for block in range(3)))
 
     def second_load(x, d=0):
         return s1[x + 2, pl.ds(2 + d, 8), :]
@@ -437,7 +562,12 @@
     u1, u2 = load(0, 1, 3), load(0, 1, 4)
     k1, k2 = minmod(q1 - q0, q2 - q1), minmod(q2 - q1, q3 - q2)
     x_low = flux(q1, k1, q2, k2, u1 + u2)
-    x_high = lax.fori_loop(0, 16, second_pair, (x_low, k2, q2, q3, u2))[0]
+    def second_group(h, carry):
+        for e in range(4):
+            carry = second_pair(4 * h + e, carry)
+        return carry
+
+    x_high = lax.fori_loop(0, 4, second_group, (x_low, k2, q2, q3, u2))[0]
     wx[...] = jnp.zeros((128, 128), F32)
     wx[pl.ds(0, 8), :] = -0.0375 * (fxs[0] + x_low)
     wx[pl.ds(8, 8), :] = 0.0375 * (fxs[16] + x_high)
@@ -466,11 +596,24 @@
         one_copy.start()
     vrecv[0] = jnp.zeros((18, 8, 128), F32)
 
-    def tail(x, carry):
+    @pl.when(row_high)
+    def _():
+        down_copy.wait_recv()
+        for f in range(2):
+            for i in range(2):
+                slab[f, NX + 2 + i, pl.ds(base_row, 8), :] = xhigh[f, i]
+
+    @pl.when(jnp.logical_not(row_high))
+    def _():
+        for f in range(2):
+            for i in range(2):
+                slab[f, NX + 2 + i] = jnp.zeros((32, 128), F32)
+
+    coarse_carry = coarse_start(62)
+    for x in (62, 63):
+        coarse_carry = coarse_plane(jnp.int32(x), coarse_carry)
+    for x in range(54, NX):
         out_c[x] = base[x]
-        return carry
-
-    lax.fori_loop(54, NX, tail, 0)
     for one_copy in back:
         one_copy.wait_recv()
     for k in range(3):
@@ -479,13 +622,26 @@
             return carry
 
         lax.fori_loop(0, 18, finish, 0)
-    for one_copy in first_copies + (patch_copy,) + tuple(back):
+    for one_copy in (box_copy, patch_copy, start_copy) + tuple(back):
         one_copy.wait_send()
+
+    @pl.when(has_side)
+    def _():
+        near_copy.wait_send()
+        far_copy.wait_send()
+
+    @pl.when(row_low)
+    def _():
+        down_copy.wait_send()
+
+    @pl.when(row_high)
+    def _():
+        up_copy.wait_send()
+        up_mate_copy.wait_send()
 
 
 def per_device(*args):
     vmem = pl.BlockSpec(memory_space=pltpu.VMEM)
-    smem = pl.BlockSpec(memory_space=pltpu.SMEM)
 
     def buf(*shape):
         return pltpu.VMEM(shape + (8, 128), F32)
@@ -496,18 +652,28 @@
             jax.ShapeDtypeStruct((64, 8, 128), F32),
             jax.ShapeDtypeStruct((32, 8, 128), F32),
         ),
-        in_specs=[vmem] * 6 + [smem] * 3,
+        in_specs=[pl.BlockSpec(memory_space=pl.ANY)] * 9,
         out_specs=(vmem, vmem),
         scratch_shapes=[
+            buf(NX),
+            buf(3, NX),
+            buf(3, NX),
+            buf(32),
+            buf(3, 32),
+            buf(3, 32),
+            pltpu.SMEM((1, args[6].shape[1]), jnp.int32),
+            pltpu.SMEM((1, args[6].shape[1]), jnp.int32),
+            pltpu.SMEM((1, args[6].shape[1]), jnp.int32),
             buf(4, NX),
             buf(4, NX),
             buf(2, 4, 2),
-            buf(4, 2),
-            buf(NX),
-            buf(2, NX),
+            buf(2, 2),
+            buf(3 * NX // 4),
+            buf(2, 3 * NX // 4),
             pltpu.VMEM((4, NX + 4, 32, 128), F32),
+            buf(WX * PACK),
+            buf(2, WX * PACK),
             buf(WX * TILES),
-            buf(2, WX * TILES),
             buf(NX),
             buf(4, 5),
             buf(4, WX * TILES),
@@ -521,11 +687,13 @@
             pltpu.VMEM((128, 128), F32),
             buf(18),
             buf(4, 18),
-            pltpu.SemaphoreType.DMA((10,)),
-            pltpu.SemaphoreType.DMA((10,)),
+            pltpu.SemaphoreType.DMA((17,)),
+            pltpu.SemaphoreType.DMA((11,)),
+            pltpu.SemaphoreType.DMA((11,)),
+            pltpu.SemaphoreType.REGULAR,
         ],
         compiler_params=pltpu.CompilerParams(
-            collective_id=0, has_side_effects=True, vmem_limit_bytes=48 * 1024 * 1024
+            collective_id=0, has_side_effects=True, vmem_limit_bytes=60 * 1024 * 1024
         ),
     )(*args)
 

time: 64.5 us -> 42.8 us (0.66)
  Pallas kernels: 54.1 us -> 39.6 us
  local copies, waits for them, and re-layouts: 9.43 us -> 2.36 us
    pallas_call x1, Pallas kernels: 54.1 us -> 39.6 us  [per_device(): pl.pallas_call(kernel, out_shape=(jax.ShapeDtypeStruct((64, 8, 128), F32)...]
    unnamed x20 -> x4, local copies, waits for them, and re-layouts: 9.43 us -> 2.36 us
where the time goes in v1:
time: 42.8 us; the launch traced here: 42.7 us
  Pallas kernels  39.6 us (93%)
  local copies, waits for them, and re-layouts  2.36 us (6%)
  between operations  0.65 us (2%)
    pallas_call x1, Pallas kernels, per_device(): pl.pallas_call(kernel, out_shape=(jax.ShapeDtypeStruct((64, 8, 128), F32)...  39.6 us
    unnamed x4, local copies, waits for them, and re-layouts  2.36 us

profile of v1, /device:TPU:1, one launch (start us, length us, event | category | flops | bytes accessed | tf_op | source)
XLA Modules:
  0.0 42.7 jit_solution(6132940110020966218)
XLA Ops:
  0.6 39.6 %shard_map.104 = (f32[64,8,128]{2,1,0:T(8,128)}, f32[32,8,128]{2,1,0:T(8,128)}) custom-call(f32[64,8,128]{2,1,0:T(8,128)} %cs_h.1, f32[3,64,8,128]{3,2,1,0:T(8,128)} %cv_h.1, f32[3,64,8,128]{3,2,1,0:T(8,128)} %cp_h.1, f32[32,8,128]{2,1,0:T(8,128)} %fs_h.1, f32[3,32,8,128]{3,2,1,0:T(8,128)} %fv_h.1, f32[3,32,8,128]{3,2,1,0:T(8,128)} %fp_h.1, ...), custom_call_target="tpu_custom_call" | custom-call | tf_op jit(solution)/shard_map/pallas_call | solution.py:649
  40.3 0.0 copy-start
  40.3 1.7 %copy.13 = f32[64,8,128]{2,1,0:T(8,128)} copy(f32[64,8,128]{2,1,0:T(8,128)} %get-tuple-element.4) | data formatting | bytes 524288
  42.0 0.0 copy-done
  42.0 0.7 %copy.14 = f32[32,8,128]{2,1,0:T(8,128)} copy(f32[32,8,128]{2,1,0:T(8,128)S(1)} %copy-done) | data formatting | bytes 262144
Async XLA Ops:
  40.3 1.7 %copy-start = (f32[32,8,128]{2,1,0:T(8,128)S(1)}, f32[32,8,128]{2,1,0:T(8,128)}, u32[]{:S(2)}) copy-start(f32[32,8,128]{2,1,0:T(8,128)} %get-tuple-element.5) | copy-start | bytes 393220

commit v2 on v1

--- a/solution.py
+++ b/solution.py
@@ -49,9 +49,9 @@
 def kernel(
     cs_h, cv_h, cp_h, fs_h, fv_h, fp_h, shift_h, offy_h, offz_h,
     out_c, out_f,
-    cs, cv, cp, fs, fv, fp, shift, offy, offz,
-    own, partner, xlow, xhigh, ysend, yrecv, slab, msend, mbuf, wide, base, masks,
-    gh, fine, s1, s1z, fxs, ry, rz, wavg, wx, vsend, vrecv,
+    cv, cp, fs, fv, fp, shift, offy, offz,
+    xlow, xhigh, ysend, yrecv, slab, msend, mbuf0, mbuf1, mbuf2, wide, base, masks,
+    gh, fine, s1, s1z, fxs, ry, rz, wavg, wx, to_zs, to_ys, vsend, vrecv,
     load_sem, send_sem, recv_sem, ready,
 ):
     rows = lax.axis_size("row")
@@ -69,12 +69,13 @@
     row_low = r > 0
     row_high = r < rows - 1
     has_side = jnp.where(core == 0, has_low, has_high)
-    out_dir = jnp.where(j_me < 2, -1, 1)
-    has_out = jnp.where(j_me < 2, has_low, has_high)
-    outer = (j_me == 0) | (j_me == 3)
-
+
+    base_row = pl.multiple_of(8 + 8 * core, 8)
+    mate_row = pl.multiple_of(16 - 8 * core, 8)
+    my_rows = pl.ds(base_row, 8)
+    mate_rows = pl.ds(mate_row, 8)
     loads = [pltpu.make_async_copy(src, dst, load_sem.at[k]) for k, (src, dst) in enumerate(
-        [(shift_h, shift), (offy_h, offy), (offz_h, offz), (cs_h, cs)]
+        [(shift_h, shift), (offy_h, offy), (offz_h, offz), (cs_h, slab.at[0, pl.ds(2, NX), my_rows])]
         + [(cv_h.at[f], cv.at[f]) for f in range(3)] + [(cp_h.at[f], cp.at[f]) for f in range(3)]
         + [(fs_h, fs)] + [(fv_h.at[f], fv.at[f]) for f in range(3)] + [(fp_h.at[f], fp.at[f]) for f in range(3)]
     )]
@@ -89,6 +90,7 @@
             bit1 = 1 - bit1
         return g0 + 2 * bit1 + bit0
 
+    near_low = g0 - 1
     near = c + sgn
     far = c + 2 * sgn
 
@@ -97,21 +99,60 @@
     def greet(*dev):
         pl.semaphore_signal(barrier, inc=1, device_id=dev, device_id_type=MESH)
 
+    above = {1: core == 0, 2: j_me < 2, 3: j_me < 2}
+    turned_up = (r == 0) & (c < 4)
+    turned_dn = (r == 1) & (c < 4)
+
     for d in (1, 2, 3):
-        greet(r, peer(d))
-
-    @pl.when(has_out)
-    def _():
-        greet(r, c + 2 * out_dir)
-
-    @pl.when(has_out & outer)
-    def _():
-        greet(r, c + out_dir)
-
-    @pl.when(row_high)
+        @pl.when(jnp.logical_not(above[d]))
+        def _(d=d):
+            greet(r, peer(d))
+
+    @pl.when((j_me < 2) & has_low)
+    def _():
+        greet(r, near_low)
+
+    @pl.when((j_me == 0) & has_low)
+    def _():
+        greet(r, c - 2)
+
+    @pl.when(row_high & jnp.logical_not(turned_up))
     def _():
         greet(r + 1, c)
         greet(r + 1, mate)
+
+    @pl.when(turned_dn)
+    def _():
+        greet(r - 1, c)
+        greet(r - 1, mate)
+
+    greeters = 3 - j_me + jnp.where(has_high & (j_me >= 2), j_me - 1, 0)
+    greeters = greeters + jnp.where(row_low & jnp.logical_not(turned_dn), 2, 0) + jnp.where(turned_up & row_high, 2, 0)
+
+    @pl.when(greeters > 0)
+    def _():
+        pl.semaphore_wait(barrier, greeters)
+
+    def answer(k, *dev):
+        pl.semaphore_signal(ready.at[k], inc=1, device_id=dev, device_id_type=MESH)
+
+    for d in (1, 2, 3):
+        @pl.when(above[d])
+        def _(d=d):
+            answer(d, r, peer(d))
+
+    @pl.when((j_me >= 2) & has_high)
+    def _():
+        answer(4, r, g0 + 4)
+
+    @pl.when(row_low & jnp.logical_not(turned_dn))
+    def _():
+        answer(0, r - 1, c)
+        answer(0, r - 1, mate)
+
+    @pl.when(turned_up & row_high)
+    def _():
+        answer(5, r + 1, c)
 
     row = tile_iota(0)
     lane = tile_iota(1)
@@ -139,10 +180,10 @@
         return acc
 
     def half_plane(x):
-        values = [cs[x]] + [0.75 * cv[f, x] - 0.25 * cp[f, x] for f in range(3)]
-        for f in range(4):
-            own[f, x] = values[f]
-        return values
+        values = [0.75 * cv[f, x] - 0.25 * cp[f, x] for f in range(3)]
+        for f in range(3):
+            slab[f + 1, x + 2, my_rows, :] = values[f]
+        return [slab[0, x + 2, my_rows, :]] + values
 
     def rows_at(value, at):
         return jnp.where(core == 0, pltpu.roll(value, at, 0) if at else value, pltpu.roll(value, (at + 2) % 8, 0))
@@ -167,33 +208,51 @@
         loads[k].wait()
     lax.fori_loop(0, NX // 4, half_coarse, 0)
 
-    greeters = 3 + jnp.where(has_out, jnp.where(outer, 2, 1), 0) + jnp.where(row_low, 2, 0)
-    pl.semaphore_wait(barrier, greeters)
-
     def copy(src, dst, k, dev, kr=None):
         return pltpu.make_async_remote_copy(
             src_ref=src, dst_ref=dst, send_sem=send_sem.at[k], recv_sem=recv_sem.at[k if kr is None else kr],
             device_id=dev, device_id_type=MESH,
         )
 
-    box_copy = copy(own, partner, 0, (r, mate))
-    up_copy = copy(own.at[:, pl.ds(NX - 2, 2)], xlow.at[0], 1, (r + 1, c))
-    up_mate_copy = copy(own.at[:, pl.ds(NX - 2, 2)], xlow.at[1], 2, (r + 1, mate))
-    down_copy = copy(own.at[pl.ds(0, 2), pl.ds(0, 2)], xhigh, 3, (r - 1, c))
+    box = slab.at[:, pl.ds(2, NX), my_rows]
+    box_copy = copy(box, box, 0, (r, mate))
+    up_copy = copy(slab.at[:, pl.ds(NX, 2), my_rows], xlow.at[0], 1, (r + 1, c))
+    up_mate_copy = copy(slab.at[:, pl.ds(NX, 2), my_rows], xlow.at[1], 2, (r + 1, mate))
+    down_copy = copy(slab.at[pl.ds(0, 2), pl.ds(2, 2), my_rows], xhigh, 3, (r - 1, c))
     near_copy = copy(ysend, yrecv.at[1 - core], 4, (r, near), 5 - core)
     far_copy = copy(ysend, yrecv.at[1 - core], 5, (r, far), 5 - core)
 
-    @pl.when(has_side)
+    @pl.when((core == 1) & has_high)
     def _():
         near_copy.start()
         far_copy.start()
 
+    @pl.when(core == 1)
+    def _():
+        pl.semaphore_wait(ready.at[1], 1)
+
     box_copy.start()
 
-    @pl.when(row_low)
-    def _():
-        pl.semaphore_signal(ready, inc=1, device_id=(r - 1, c), device_id_type=MESH)
-        pl.semaphore_signal(ready, inc=1, device_id=(r - 1, mate), device_id_type=MESH)
+    @pl.when((j_me == 0) & has_low)
+    def _():
+        pl.semaphore_wait(ready.at[4], 2)
+        near_copy.start()
+        far_copy.start()
+
+    @pl.when(j_me == 2)
+    def _():
+        pl.semaphore_wait(ready.at[3], 1)
+        near_copy.start()
+        pl.semaphore_wait(ready.at[2], 1)
+        far_copy.start()
+
+    @pl.when(turned_up & row_high)
+    def _():
+        up_copy.start()
+        up_mate_copy.start()
+
+    @pl.when(row_low & jnp.logical_not(turned_dn))
+    def _():
         down_copy.start()
 
     def half_fine(x, carry):
@@ -229,8 +288,6 @@
     for q in range(5):
         masks[3, q] = jnp.zeros((8, 128), F32)
 
-    base_row = pl.multiple_of(8 + 8 * core, 8)
-    mate_row = pl.multiple_of(16 - 8 * core, 8)
 
     @pl.when(has_low)
     def _():
@@ -245,14 +302,15 @@
         def _(side=side):
             yrecv[side] = jnp.zeros((3 * NX // 4, 8, 128), F32)
 
-    box_copy.wait_recv()
+    @pl.when(row_high & jnp.logical_not(turned_up))
+    def _():
+        pl.semaphore_wait(ready.at[0], 2)
+        up_copy.start()
+        up_mate_copy.start()
 
     def assemble(h, carry):
         for e in range(4):
             x = 4 * h + e
-            for f in range(4):
-                slab[f, x + 2, pl.ds(base_row, 8), :] = own[f, x]
-                slab[f, x + 2, pl.ds(mate_row, 8), :] = partner[f, x]
             for side, at in ((0, 6), (1, 24)):
                 pair = 3 * h + e // 2
                 slab[0, x + 2, pl.ds(at, 2), :] = yrecv[side, pair, pl.ds(4 * (e % 2), 2), :]
@@ -263,14 +321,15 @@
         return carry
 
     lax.fori_loop(0, NX // 4, assemble, 0)
-
-    def extractor(t, store):
+    box_copy.wait_recv()
+
+    def extractor(t):
         p = pick(par, t)
         first = 18 * pick(rank, t)
         r0 = 5 + 8 * lax.rem(p, 2) + pick(oyv, t)
         turn = 131 - pick(ozv, t)
 
-        def plane(i, carry):
+        def plane(i, put):
             x = first + i
 
             def rolled(value, to):
@@ -284,34 +343,48 @@
             rest = rolled(edge, 0)
             for f in range(4):
                 rest = jnp.where(lane >= 96 + 8 * f, rolled(four[f], 32 + 8 * f), rest)
-            store(PACK * i, jnp.where(lane < 64, rolled(four[0], 0), rolled(four[1], 64)))
-            store(PACK * i + 1, jnp.where(lane < 64, rolled(four[2], 0), rolled(four[3], 64)))
-            store(PACK * i + 2, rest)
+            put(0, jnp.where(lane < 64, rolled(four[0], 0), rolled(four[1], 64)))
+            put(1, jnp.where(lane < 64, rolled(four[2], 0), rolled(four[3], 64)))
+            put(2, rest)
+
+        return plane
+
+    cross = extractor(lax.rem(j_me + 2, 4))
+    mine = extractor(j_me)
+    chunks = ((2, 12), (12, WX), (0, 2))
+    mbufs = (mbuf0, mbuf1, mbuf2)
+
+    def extract(k, plane, own):
+        at, end = chunks[k]
+
+        def step(i, carry):
+            def put(q, value):
+                if own:
+                    mbufs[k][0, PACK * (i - at) + q] = value
+                else:
+                    msend[PACK * i + q] = value
+
+            plane(i, put)
             return carry
 
-        return plane
-
-    def store_send(k, value):
-        msend[k] = value
-
-    def store_own(k, value):
-        mbuf[0, k] = value
-
-    cut = 2 * PACK
-    size = (WX - 2) * PACK
-    cross = extractor(lax.rem(j_me + 2, 4), store_send)
-    lax.fori_loop(2, WX, cross, 0, unroll=4)
-    patch_copy = copy(msend.at[pl.ds(cut, size)], mbuf.at[1, pl.ds(cut, size)], 6, (r, peer(2)))
-    patch_copy.start()
-
-    @pl.when(row_high)
-    def _():
-        pl.semaphore_wait(ready, 2)
-        up_copy.start()
-        up_mate_copy.start()
-
-    mine = extractor(j_me, store_own)
-    lax.fori_loop(2, WX, mine, 0, unroll=4)
+        lax.fori_loop(at, end, step, 0, unroll=min(5, end - at))
+
+    def chunk_copy(k):
+        at, end = chunks[k]
+        return copy(msend.at[pl.ds(PACK * at, PACK * (end - at))], mbufs[k].at[1], (6, 10, 11)[k], (r, peer(2)))
+
+    patch_copies = [chunk_copy(k) for k in range(3)]
+    extract(0, cross, False)
+
+    @pl.when(j_me == 3)
+    def _():
+        pl.semaphore_wait(ready.at[2], 1)
+
+    patch_copies[0].start()
+    extract(1, cross, False)
+    patch_copies[1].start()
+    extract(0, mine, True)
+    extract(1, mine, True)
 
     @pl.when(row_low)
     def _():
@@ -328,12 +401,9 @@
             for i in range(2):
                 slab[f, i] = jnp.zeros((32, 128), F32)
 
-    for i in range(2):
-        cross(i, 0)
-    start_copy = copy(msend.at[pl.ds(0, cut)], mbuf.at[1, pl.ds(0, cut)], 10, (r, peer(2)))
-    start_copy.start()
-    for i in range(2):
-        mine(i, 0)
+    extract(2, cross, False)
+    patch_copies[2].start()
+    extract(2, mine, True)
 
     def coarse_load(f, x, delta=0):
         return slab[f, x, pl.ds(base_row + delta, 8), :]
@@ -379,9 +449,12 @@
         m1, m2 = minmod(p1 - p0, p2 - p1), minmod(p2 - p1, p3 - p2)
         return flux(p1, m1, p2, m2, v1 + v2), m2, p2, p3, v2
 
-    coarse_carry = lax.fori_loop(0, 10, coarse_group, coarse_start(0))
-    for x in (60, 61):
-        coarse_carry = coarse_plane(jnp.int32(x), coarse_carry)
+    lax.fori_loop(0, 5, coarse_group, coarse_start(0))
+
+    @pl.when(turned_dn)
+    def _():
+        pl.semaphore_wait(ready.at[5], 1)
+        down_copy.start()
 
     my_par = pick(par, j_me)
     my_oy = pick(oyv, j_me)
@@ -398,23 +471,33 @@
     zmat = jnp.where(zi == cell, 1.0, 0.0) + jnp.where(zi == cell + 1, slope, 0.0) - jnp.where(zi == cell - 1, slope, 0.0)
     zmat = zmat.astype(jnp.bfloat16)
 
-    patch_copy.wait_recv()
-    start_copy.wait_recv()
-
-    def unpack(i, carry):
-        first, second, rest = [mbuf[sel, PACK * i + q] for q in range(PACK)]
-        for f, value in enumerate((first, pltpu.roll(first, 64, 1), second, pltpu.roll(second, 64, 1))):
-            wide[TILES * i + f] = jnp.where(lane < 64, value, pltpu.roll(rest, 96 - 8 * f, 1))
-        wide[TILES * i + 4] = rest
-        return carry
-
-    lax.fori_loop(0, WX, unpack, 0, unroll=2)
-    half = WX * TILES // 2
-    for h in range(2):
-        lhs = wide[pl.ds(h * half, half)].reshape(half * 8, 128)
-        res = split_dot(lhs, zmat)
+    ri = lax.broadcasted_iota(jnp.int32, (128, 128), 0)
+    ci = lax.broadcasted_iota(jnp.int32, (128, 128), 1)
+    to_zs[0] = jnp.where(ci == my_oz + (ri >> 1), 1.0, 0.0).astype(jnp.bfloat16)
+    to_zface = jnp.where((ri == 127) & (ci == my_oz + 64), 1.0, 0.0) - jnp.where((ri == 0) & (ci == my_oz - 1), 1.0, 0.0)
+    to_zs[1] = to_zface.astype(jnp.bfloat16)
+    same = (ri >> 3) == (ci >> 3)
+    yr, yc = ri & 7, ci & 7
+    to_ys[0] = jnp.where(same & (yr == my_oy + (yc >> 1)), 1.0, 0.0).astype(jnp.bfloat16)
+    to_yface = jnp.where(same & (yc == 7) & (yr == my_oy + 4), 1.0, 0.0) - jnp.where(same & (yc == 0) & (yr == my_oy - 1), 1.0, 0.0)
+    to_ys[1] = to_yface.astype(jnp.bfloat16)
+
+    def unpack_chunk(k):
+        at, end = chunks[k]
+        patch_copies[k].wait_recv()
+
+        def unpack(i, carry):
+            first, second, rest = [mbufs[k][sel, PACK * (i - at) + q] for q in range(PACK)]
+            for f, value in enumerate((first, pltpu.roll(first, 64, 1), second, pltpu.roll(second, 64, 1))):
+                wide[TILES * i + f] = jnp.where(lane < 64, value, pltpu.roll(rest, 96 - 8 * f, 1))
+            wide[TILES * i + 4] = rest
+            return carry
+
+        lax.fori_loop(at, end, unpack, 0, unroll=min(5, end - at))
+        part, size = pl.ds(TILES * at, TILES * (end - at)), TILES * (end - at)
+        res = split_dot(wide[part].reshape(size * 8, 128), zmat)
         for q in range(4):
-            gh[q, pl.ds(h * half, half)] = res[:, 128 * q:128 * (q + 1)].reshape(half, 8, 128)
+            gh[q, part] = res[:, 128 * q:128 * (q + 1)].reshape(size, 8, 128)
 
     def refine_plane(i, full):
         for lt in range(2):
@@ -443,16 +526,12 @@
                             fine[f, lt, xf, pl.ds(ey, 2, stride=2), :] = value[0:2]
                             fine[f, lt, xf, pl.ds(12 + ey, 2, stride=2), :] = value[6:8]
 
-    def refine_ends(i, carry):
-        refine_plane(jnp.where(i < 2, i + 1, i + 17), True)
-        return carry
-
-    def refine_middle(i, carry):
-        refine_plane(i, False)
-        return carry
-
-    lax.fori_loop(0, 4, refine_ends, 0)
-    lax.fori_loop(3, 19, refine_middle, 0)
+    def refine(at, end, full):
+        def step(i, carry):
+            refine_plane(i, full)
+            return carry
+
+        lax.fori_loop(at, end, step, 0)
 
     def zup(t0, t1):
         a0, a1 = pltpu.roll(t0, 127, 1), pltpu.roll(t1, 127, 1)
@@ -526,11 +605,20 @@
         return carries
 
     def first_group(h, carries):
-        for e in range(3):
-            carries = first_pair(3 * h + e, carries)
+        for e in range(2):
+            carries = first_pair(2 * h + e, carries)
         return carries
 
-    lax.fori_loop(0, 6, first_group, tuple(x_start(block, 2) for block in range(3)))
+    unpack_chunk(0)
+    refine(3, 11, False)
+    carries = lax.fori_loop(1, 4, first_group, tuple(x_start(block, 6) for block in range(3)))
+    unpack_chunk(1)
+    refine(11, 19, False)
+    refine(19, 21, True)
+    lax.fori_loop(4, 9, first_group, carries)
+    unpack_chunk(2)
+    refine(1, 3, True)
+    first_group(0, tuple(x_start(block, 2) for block in range(3)))
 
     def second_load(x, d=0):
         return s1[x + 2, pl.ds(2 + d, 8), :]
@@ -567,34 +655,40 @@
             carry = second_pair(4 * h + e, carry)
         return carry
 
-    x_high = lax.fori_loop(0, 4, second_group, (x_low, k2, q2, q3, u2))[0]
-    wx[...] = jnp.zeros((128, 128), F32)
+    def place(at, count):
+        part = pl.ds(8 * at, 8 * count)
+        to_y, to_yface = to_ys[0, 0:8 * count, 0:8 * count], to_ys[1, 0:8 * count, 0:8 * count]
+        placed = split_dot(wavg[0, part], to_zs[0]) + split_dot(wavg[1, part], to_zs[1])
+        faces = split_dot(wavg[2, part], to_zs[0])
+        middle = split_dot_left(to_y, placed) + split_dot_left(to_yface, faces)
+        vsend[pl.ds(at, count)] = middle.reshape(count, 8, 128)
+
+    @pl.when(j_me == 3)
+    def _():
+        pl.semaphore_wait(ready.at[3], 1)
+
+    def back_copy(d, k):
+        part = pl.ds(8 * k, 8 + 2 * k)
+        return copy(vsend.at[part], vrecv.at[d, part], 6 + d if k == 0 else 11 + d, (r, peer(d)))
+
+    back = [[back_copy(d, k) for d in (2, 3, 1)] for k in range(2)]
+    carry = lax.fori_loop(0, 2, second_group, (x_low, k2, q2, q3, u2))
+    place(0, 8)
+    for one_copy in back[0]:
+        one_copy.start()
+    x_high = lax.fori_loop(2, 4, second_group, carry)[0]
     wx[pl.ds(0, 8), :] = -0.0375 * (fxs[0] + x_low)
     wx[pl.ds(8, 8), :] = 0.0375 * (fxs[16] + x_high)
-
-    ri = lax.broadcasted_iota(jnp.int32, (128, 128), 0)
-    ci = lax.broadcasted_iota(jnp.int32, (128, 128), 1)
-    to_z = jnp.where(ci == my_oz + (ri >> 1), 1.0, 0.0).astype(jnp.bfloat16)
-    to_zface = jnp.where((ri == 127) & (ci == my_oz + 64), 1.0, 0.0) - jnp.where((ri == 0) & (ci == my_oz - 1), 1.0, 0.0)
-    to_zface = to_zface.astype(jnp.bfloat16)
-    same = (ri >> 3) == (ci >> 3)
-    yr, yc = ri & 7, ci & 7
-    to_y = jnp.where(same & (yr == my_oy + (yc >> 1)), 1.0, 0.0).astype(jnp.bfloat16)
-    to_yface = jnp.where(same & (yc == 7) & (yr == my_oy + 4), 1.0, 0.0) - jnp.where(same & (yc == 0) & (yr == my_oy - 1), 1.0, 0.0)
-    to_yface = to_yface.astype(jnp.bfloat16)
-    placed = split_dot(wavg[0], to_z) + split_dot(wavg[1], to_zface)
-    faces = split_dot(wavg[2], to_z)
-    ends = split_dot(wx[...], to_z)
-    middle = split_dot_left(to_y, placed) + split_dot_left(to_yface, faces)
-    ends = split_dot_left(to_y, ends)
-    vsend[pl.ds(1, 16)] = middle.reshape(16, 8, 128)
-    vsend[0] = ends[0:8]
-    vsend[17] = ends[8:16]
-
-    back = [copy(vsend, vrecv.at[d], 6 + d, (r, peer(d))) for d in (1, 2, 3)]
-    for one_copy in back:
+    place(8, 8)
+    vsend[pl.ds(16, 2)] = split_dot_left(to_ys[0, 0:16, 0:16], split_dot(wx[...], to_zs[0])).reshape(2, 8, 128)
+    for one_copy in back[1]:
         one_copy.start()
+    back = back[0] + back[1]
     vrecv[0] = jnp.zeros((18, 8, 128), F32)
+
+    coarse_carry = lax.fori_loop(5, 10, coarse_group, coarse_start(30))
+    for x in (60, 61):
+        coarse_carry = coarse_plane(jnp.int32(x), coarse_carry)
 
     @pl.when(row_high)
     def _():
@@ -609,7 +703,6 @@
             for i in range(2):
                 slab[f, NX + 2 + i] = jnp.zeros((32, 128), F32)
 
-    coarse_carry = coarse_start(62)
     for x in (62, 63):
         coarse_carry = coarse_plane(jnp.int32(x), coarse_carry)
     for x in range(54, NX):
@@ -618,11 +711,13 @@
         one_copy.wait_recv()
     for k in range(3):
         def finish(i, carry, k=k):
-            out_c[18 * k + i] = base[18 * k + i] + vrecv[slots[k], i]
+            out_c[18 * k + 1 + i] = base[18 * k + 1 + i] + vrecv[slots[k], i]
             return carry
 
-        lax.fori_loop(0, 18, finish, 0)
-    for one_copy in (box_copy, patch_copy, start_copy) + tuple(back):
+        lax.fori_loop(0, 16, finish, 0, unroll=8)
+        for x, i in ((18 * k, 16), (18 * k + 17, 17)):
+            out_c[x] = base[x] + vrecv[slots[k], i]
+    for one_copy in [box_copy] + patch_copies + back:
         one_copy.wait_send()
 
     @pl.when(has_side)
@@ -655,7 +750,6 @@
         in_specs=[pl.BlockSpec(memory_space=pl.ANY)] * 9,
         out_specs=(vmem, vmem),
         scratch_shapes=[
-            buf(NX),
             buf(3, NX),
             buf(3, NX),
             buf(32),
@@ -664,15 +758,15 @@
             pltpu.SMEM((1, args[6].shape[1]), jnp.int32),
             pltpu.SMEM((1, args[6].shape[1]), jnp.int32),
             pltpu.SMEM((1, args[6].shape[1]), jnp.int32),
-            buf(4, NX),
-            buf(4, NX),
             buf(2, 4, 2),
             buf(2, 2),
             buf(3 * NX // 4),
             buf(2, 3 * NX // 4),
             pltpu.VMEM((4, NX + 4, 32, 128), F32),
             buf(WX * PACK),
-            buf(2, WX * PACK),
+            buf(2, 10 * PACK),
+            buf(2, 10 * PACK),
+            buf(2, 2 * PACK),
             buf(WX * TILES),
             buf(NX),
             buf(4, 5),
@@ -684,13 +778,15 @@
             buf(18),
             buf(18),
             pltpu.VMEM((3, 128, 128), F32),
-            pltpu.VMEM((128, 128), F32),
+            pltpu.VMEM((16, 128), F32),
+            pltpu.VMEM((2, 128, 128), jnp.bfloat16),
+            pltpu.VMEM((2, 128, 128), jnp.bfloat16),
             buf(18),
             buf(4, 18),
             pltpu.SemaphoreType.DMA((17,)),
-            pltpu.SemaphoreType.DMA((11,)),
-            pltpu.SemaphoreType.DMA((11,)),
-            pltpu.SemaphoreType.REGULAR,
+            pltpu.SemaphoreType.DMA((15,)),
+            pltpu.SemaphoreType.DMA((15,)),
+            pltpu.SemaphoreType.REGULAR((6,)),
         ],
         compiler_params=pltpu.CompilerParams(
             collective_id=0, has_side_effects=True, vmem_limit_bytes=60 * 1024 * 1024

time: 42.8 us -> 39 us (0.911)
  Pallas kernels: 39.6 us -> 35.8 us
    pallas_call x1, Pallas kernels: 39.6 us -> 35.8 us  [per_device(): pl.pallas_call(kernel, out_shape=(jax.ShapeDtypeStruct((64, 8, 128), F32)...]
where the time goes in v2:
time: 39 us; the launch traced here: 38.9 us
  Pallas kernels  35.8 us (92%)
  local copies, waits for them, and re-layouts  2.36 us (6%)
  between operations  0.65 us (2%)
    pallas_call x1, Pallas kernels, per_device(): pl.pallas_call(kernel, out_shape=(jax.ShapeDtypeStruct((64, 8, 128), F32)...  35.8 us
    unnamed x4, local copies, waits for them, and re-layouts  2.36 us

profile of v2, /device:TPU:1, one launch (start us, length us, event | category | flops | bytes accessed | tf_op | source)
XLA Modules:
  0.0 38.9 jit_solution(13864959354035417667)
XLA Ops:
  0.6 35.8 %shard_map.104 = (f32[64,8,128]{2,1,0:T(8,128)}, f32[32,8,128]{2,1,0:T(8,128)}) custom-call(f32[64,8,128]{2,1,0:T(8,128)} %cs_h.1, f32[3,64,8,128]{3,2,1,0:T(8,128)} %cv_h.1, f32[3,64,8,128]{3,2,1,0:T(8,128)} %cp_h.1, f32[32,8,128]{2,1,0:T(8,128)} %fs_h.1, f32[3,32,8,128]{3,2,1,0:T(8,128)} %fv_h.1, f32[3,32,8,128]{3,2,1,0:T(8,128)} %fp_h.1, ...), custom_call_target="tpu_custom_call" | custom-call | tf_op jit(solution)/shard_map/pallas_call | solution.py:744
  36.5 0.0 copy-start
  36.5 1.7 %copy.13 = f32[64,8,128]{2,1,0:T(8,128)} copy(f32[64,8,128]{2,1,0:T(8,128)} %get-tuple-element.4) | data formatting | bytes 524288
  38.2 0.0 copy-done
  38.2 0.7 %copy.14 = f32[32,8,128]{2,1,0:T(8,128)} copy(f32[32,8,128]{2,1,0:T(8,128)S(1)} %copy-done) | data formatting | bytes 262144
Async XLA Ops:
  36.5 1.7 %copy-start = (f32[32,8,128]{2,1,0:T(8,128)S(1)}, f32[32,8,128]{2,1,0:T(8,128)}, u32[]{:S(2)}) copy-start(f32[32,8,128]{2,1,0:T(8,128)} %get-tuple-element.5) | copy-start | bytes 393220

commit v3 on v2

--- a/solution.py
+++ b/solution.py
@@ -10,7 +10,7 @@
 NX = 64
 WX = 22
 TILES = 5
-PACK = 3
+PACK = 5
 
 
 def minmod(p, q):
@@ -74,11 +74,14 @@
     mate_row = pl.multiple_of(16 - 8 * core, 8)
     my_rows = pl.ds(base_row, 8)
     mate_rows = pl.ds(mate_row, 8)
-    loads = [pltpu.make_async_copy(src, dst, load_sem.at[k]) for k, (src, dst) in enumerate(
-        [(shift_h, shift), (offy_h, offy), (offz_h, offz), (cs_h, slab.at[0, pl.ds(2, NX), my_rows])]
-        + [(cv_h.at[f], cv.at[f]) for f in range(3)] + [(cp_h.at[f], cp.at[f]) for f in range(3)]
-        + [(fs_h, fs)] + [(fv_h.at[f], fv.at[f]) for f in range(3)] + [(fp_h.at[f], fp.at[f]) for f in range(3)]
-    )]
+    half = NX // 2
+    pairs = [(shift_h, shift), (offy_h, offy), (offz_h, offz)]
+    for h in range(2):
+        xs = pl.ds(half * h, half)
+        pairs.append((cs_h.at[xs], slab.at[0, pl.ds(2 + half * h, half), my_rows]))
+        pairs += [(cv_h.at[f, xs], cv.at[f, xs]) for f in range(3)] + [(cp_h.at[f, xs], cp.at[f, xs]) for f in range(3)]
+    pairs += [(fs_h, fs)] + [(fv_h.at[f], fv.at[f]) for f in range(3)] + [(fp_h.at[f], fp.at[f]) for f in range(3)]
+    loads = [pltpu.make_async_copy(src, dst, load_sem.at[k]) for k, (src, dst) in enumerate(pairs)]
     for load_copy in loads:
         load_copy.start()
 
@@ -90,9 +93,7 @@
             bit1 = 1 - bit1
         return g0 + 2 * bit1 + bit0
 
-    near_low = g0 - 1
     near = c + sgn
-    far = c + 2 * sgn
 
     barrier = pltpu.get_barrier_semaphore()
 
@@ -108,13 +109,9 @@
         def _(d=d):
             greet(r, peer(d))
 
-    @pl.when((j_me < 2) & has_low)
-    def _():
-        greet(r, near_low)
-
     @pl.when((j_me == 0) & has_low)
     def _():
-        greet(r, c - 2)
+        greet(r, c - 1)
 
     @pl.when(row_high & jnp.logical_not(turned_up))
     def _():
@@ -126,7 +123,7 @@
         greet(r - 1, c)
         greet(r - 1, mate)
 
-    greeters = 3 - j_me + jnp.where(has_high & (j_me >= 2), j_me - 1, 0)
+    greeters = 3 - j_me + jnp.where(has_high & (j_me == 3), 1, 0)
     greeters = greeters + jnp.where(row_low & jnp.logical_not(turned_dn), 2, 0) + jnp.where(turned_up & row_high, 2, 0)
 
     @pl.when(greeters > 0)
@@ -141,9 +138,9 @@
         def _(d=d):
             answer(d, r, peer(d))
 
-    @pl.when((j_me >= 2) & has_high)
-    def _():
-        answer(4, r, g0 + 4)
+    @pl.when((j_me == 3) & has_high)
+    def _():
+        answer(4, r, c + 1)
 
     @pl.when(row_low & jnp.logical_not(turned_dn))
     def _():
@@ -204,47 +201,52 @@
         ysend[3 * h + 2] = tile
         return carry
 
-    for k in range(3, 10):
-        loads[k].wait()
-    lax.fori_loop(0, NX // 4, half_coarse, 0)
-
     def copy(src, dst, k, dev, kr=None):
         return pltpu.make_async_remote_copy(
             src_ref=src, dst_ref=dst, send_sem=send_sem.at[k], recv_sem=recv_sem.at[k if kr is None else kr],
             device_id=dev, device_id_type=MESH,
         )
 
-    box = slab.at[:, pl.ds(2, NX), my_rows]
-    box_copy = copy(box, box, 0, (r, mate))
+    boxes = [slab.at[:, pl.ds(2 + half * h, half), my_rows] for h in range(2)]
+    box_copies = [copy(boxes[h], boxes[h], 15 * h, (r, mate)) for h in range(2)]
+    for k in range(3, 10):
+        loads[k].wait()
+    lax.fori_loop(0, NX // 8, half_coarse, 0)
+
+    @pl.when(core == 0)
+    def _():
+        box_copies[0].start()
+
+    for k in range(10, 17):
+        loads[k].wait()
+    lax.fori_loop(NX // 8, NX // 4, half_coarse, 0)
+
     up_copy = copy(slab.at[:, pl.ds(NX, 2), my_rows], xlow.at[0], 1, (r + 1, c))
     up_mate_copy = copy(slab.at[:, pl.ds(NX, 2), my_rows], xlow.at[1], 2, (r + 1, mate))
     down_copy = copy(slab.at[pl.ds(0, 2), pl.ds(2, 2), my_rows], xhigh, 3, (r - 1, c))
     near_copy = copy(ysend, yrecv.at[1 - core], 4, (r, near), 5 - core)
-    far_copy = copy(ysend, yrecv.at[1 - core], 5, (r, far), 5 - core)
+    hand_copy = copy(yrecv.at[core], yrecv.at[core], 5, (r, mate), 4 + core)
 
     @pl.when((core == 1) & has_high)
     def _():
         near_copy.start()
-        far_copy.start()
 
     @pl.when(core == 1)
     def _():
         pl.semaphore_wait(ready.at[1], 1)
-
-    box_copy.start()
+        box_copies[0].start()
+
+    box_copies[1].start()
 
     @pl.when((j_me == 0) & has_low)
     def _():
-        pl.semaphore_wait(ready.at[4], 2)
+        pl.semaphore_wait(ready.at[4], 1)
         near_copy.start()
-        far_copy.start()
 
     @pl.when(j_me == 2)
     def _():
         pl.semaphore_wait(ready.at[3], 1)
         near_copy.start()
-        pl.semaphore_wait(ready.at[2], 1)
-        far_copy.start()
 
     @pl.when(turned_up & row_high)
     def _():
@@ -261,7 +263,7 @@
             fine[f + 1, 0, x + 4, pl.ds(4, 8), :] = 0.75 * fv[f, x] - 0.25 * fp[f, x]
         return carry
 
-    for k in range(10, 17):
+    for k in range(17, 24):
         loads[k].wait()
     lax.fori_loop(0, 32, half_fine, 0, unroll=4)
 
@@ -289,13 +291,14 @@
         masks[3, q] = jnp.zeros((8, 128), F32)
 
 
-    @pl.when(has_low)
-    def _():
-        copy(ysend, yrecv.at[0], 4, (r, mate)).wait_recv()
-
-    @pl.when(has_high)
-    def _():
-        copy(ysend, yrecv.at[1], 5, (r, mate)).wait_recv()
+    @pl.when(has_side)
+    def _():
+        copy(ysend, yrecv.at[core], 4, (r, near), 4 + core).wait_recv()
+        hand_copy.start()
+
+    @pl.when(jnp.where(core == 0, has_high, has_low))
+    def _():
+        copy(yrecv.at[1 - core], yrecv.at[1 - core], 5, (r, mate), 5 - core).wait_recv()
 
     for side, has in ((0, has_low), (1, has_high)):
         @pl.when(jnp.logical_not(has))
@@ -321,7 +324,8 @@
         return carry
 
     lax.fori_loop(0, NX // 4, assemble, 0)
-    box_copy.wait_recv()
+    for one_copy in box_copies:
+        one_copy.wait_recv()
 
     def extractor(t):
         p = pick(par, t)
@@ -329,54 +333,58 @@
         r0 = 5 + 8 * lax.rem(p, 2) + pick(oyv, t)
         turn = 131 - pick(ozv, t)
 
-        def plane(i, put):
-            x = first + i
-
+        def pair(h, put):
             def rolled(value, to):
                 return pltpu.roll(value, lax.rem(turn + to, 128), 1)
 
-            four = [slab[f, x, pl.ds(r0 + 1, 8), :] for f in range(4)]
-            edge = slab[0, x, pl.ds(r0, 8), :]
-            edge = jnp.where(row == 7, slab[0, x, pl.ds(r0 + 2, 8), :], edge)
-            edge = jnp.where(row == 1, slab[2, x, pl.ds(r0 - 1, 8), :], edge)
-            edge = jnp.where(row == 6, slab[2, x, pl.ds(r0 + 3, 8), :], edge)
-            rest = rolled(edge, 0)
-            for f in range(4):
-                rest = jnp.where(lane >= 96 + 8 * f, rolled(four[f], 32 + 8 * f), rest)
-            put(0, jnp.where(lane < 64, rolled(four[0], 0), rolled(four[1], 64)))
-            put(1, jnp.where(lane < 64, rolled(four[2], 0), rolled(four[3], 64)))
-            put(2, rest)
-
-        return plane
+            rest = []
+            for e in range(2):
+                x = first + 2 * h + e
+                four = [slab[f, x, pl.ds(r0 + 1, 8), :] for f in range(4)]
+                edge = slab[0, x, pl.ds(r0, 8), :]
+                edge = jnp.where(row == 7, slab[0, x, pl.ds(r0 + 2, 8), :], edge)
+                edge = jnp.where(row == 1, slab[2, x, pl.ds(r0 - 1, 8), :], edge)
+                edge = jnp.where(row == 6, slab[2, x, pl.ds(r0 + 3, 8), :], edge)
+                rest.append((rolled(edge, 0), four))
+                put(2 * e, jnp.where(lane < 64, rolled(four[0], 0), rolled(four[1], 64)))
+                put(2 * e + 1, jnp.where(lane < 64, rolled(four[2], 0), rolled(four[3], 64)))
+            both = jnp.where((row < 2) | (row >= 6), rest[0][0], jnp.where(row < 4, pltpu.roll(rest[1][0], 2, 0), pltpu.roll(rest[1][0], 6, 0)))
+            for e in range(2):
+                for f in range(4):
+                    at = 72 + 24 * e + 6 * f
+                    both = jnp.where(lane >= at, rolled(rest[e][1][f], at - 64), both)
+            put(4, both)
+
+        return pair
 
     cross = extractor(lax.rem(j_me + 2, 4))
     mine = extractor(j_me)
-    chunks = ((2, 12), (12, WX), (0, 2))
+    chunks = ((2, 14), (14, WX), (0, 2))
     mbufs = (mbuf0, mbuf1, mbuf2)
 
-    def extract(k, plane, own):
-        at, end = chunks[k]
-
-        def step(i, carry):
+    def extract(k, pair, own):
+        at, end = chunks[k][0] // 2, chunks[k][1] // 2
+
+        def step(h, carry):
             def put(q, value):
                 if own:
-                    mbufs[k][0, PACK * (i - at) + q] = value
+                    mbufs[k][0, PACK * (h - at) + q] = value
                 else:
-                    msend[PACK * i + q] = value
-
-            plane(i, put)
+                    msend[PACK * h + q] = value
+
+            pair(h, put)
             return carry
 
-        lax.fori_loop(at, end, step, 0, unroll=min(5, end - at))
+        lax.fori_loop(at, end, step, 0, unroll=min(2, end - at))
 
     def chunk_copy(k):
-        at, end = chunks[k]
+        at, end = chunks[k][0] // 2, chunks[k][1] // 2
         return copy(msend.at[pl.ds(PACK * at, PACK * (end - at))], mbufs[k].at[1], (6, 10, 11)[k], (r, peer(2)))
 
     patch_copies = [chunk_copy(k) for k in range(3)]
     extract(0, cross, False)
 
-    @pl.when(j_me == 3)
+    @pl.when(j_me >= 2)
     def _():
         pl.semaphore_wait(ready.at[2], 1)
 
@@ -486,14 +494,18 @@
         at, end = chunks[k]
         patch_copies[k].wait_recv()
 
-        def unpack(i, carry):
-            first, second, rest = [mbufs[k][sel, PACK * (i - at) + q] for q in range(PACK)]
-            for f, value in enumerate((first, pltpu.roll(first, 64, 1), second, pltpu.roll(second, 64, 1))):
-                wide[TILES * i + f] = jnp.where(lane < 64, value, pltpu.roll(rest, 96 - 8 * f, 1))
-            wide[TILES * i + 4] = rest
+        def unpack(h, carry):
+            tiles = [mbufs[k][sel, PACK * (h - at // 2) + q] for q in range(PACK)]
+            rest = tiles[4]
+            for e in range(2):
+                first, second = tiles[2 * e], tiles[2 * e + 1]
+                to = TILES * (2 * h + e)
+                for f, value in enumerate((first, pltpu.roll(first, 64, 1), second, pltpu.roll(second, 64, 1))):
+                    wide[to + f] = jnp.where(lane < 64, value, pltpu.roll(rest, (120 - 24 * e - 6 * f) % 128, 1))
+                wide[to + 4] = jnp.where(row < 4, pltpu.roll(rest, 6, 0), pltpu.roll(rest, 2, 0)) if e else rest
             return carry
 
-        lax.fori_loop(at, end, unpack, 0, unroll=min(5, end - at))
+        lax.fori_loop(at // 2, end // 2, unpack, 0, unroll=min(2, (end - at) // 2))
         part, size = pl.ds(TILES * at, TILES * (end - at)), TILES * (end - at)
         res = split_dot(wide[part].reshape(size * 8, 128), zmat)
         for q in range(4):
@@ -610,12 +622,12 @@
         return carries
 
     unpack_chunk(0)
-    refine(3, 11, False)
-    carries = lax.fori_loop(1, 4, first_group, tuple(x_start(block, 6) for block in range(3)))
+    refine(3, 13, False)
+    carries = lax.fori_loop(1, 5, first_group, tuple(x_start(block, 6) for block in range(3)))
     unpack_chunk(1)
-    refine(11, 19, False)
+    refine(13, 19, False)
     refine(19, 21, True)
-    lax.fori_loop(4, 9, first_group, carries)
+    lax.fori_loop(5, 9, first_group, carries)
     unpack_chunk(2)
     refine(1, 3, True)
     first_group(0, tuple(x_start(block, 2) for block in range(3)))
@@ -717,13 +729,13 @@
         lax.fori_loop(0, 16, finish, 0, unroll=8)
         for x, i in ((18 * k, 16), (18 * k + 17, 17)):
             out_c[x] = base[x] + vrecv[slots[k], i]
-    for one_copy in [box_copy] + patch_copies + back:
+    for one_copy in box_copies + patch_copies + back:
         one_copy.wait_send()
 
     @pl.when(has_side)
     def _():
         near_copy.wait_send()
-        far_copy.wait_send()
+        hand_copy.wait_send()
 
     @pl.when(row_low)
     def _():
@@ -763,10 +775,10 @@
             buf(3 * NX // 4),
             buf(2, 3 * NX // 4),
             pltpu.VMEM((4, NX + 4, 32, 128), F32),
-            buf(WX * PACK),
-            buf(2, 10 * PACK),
-            buf(2, 10 * PACK),
-            buf(2, 2 * PACK),
+            buf(WX // 2 * PACK),
+            buf(2, 6 * PACK),
+            buf(2, 4 * PACK),
+            buf(2, PACK),
             buf(WX * TILES),
             buf(NX),
             buf(4, 5),
@@ -783,9 +795,9 @@
             pltpu.VMEM((2, 128, 128), jnp.bfloat16),
             buf(18),
             buf(4, 18),
-            pltpu.SemaphoreType.DMA((17,)),
-            pltpu.SemaphoreType.DMA((15,)),
-            pltpu.SemaphoreType.DMA((15,)),
+            pltpu.SemaphoreType.DMA((24,)),
+            pltpu.SemaphoreType.DMA((16,)),
+            pltpu.SemaphoreType.DMA((16,)),
             pltpu.SemaphoreType.REGULAR((6,)),
         ],
         compiler_params=pltpu.CompilerParams(

time: 39 us -> 38.1 us (0.977)
  Pallas kernels: 35.8 us -> 34.9 us
    pallas_call x1, Pallas kernels: 35.8 us -> 34.9 us  [per_device(): pl.pallas_call(kernel, out_shape=(jax.ShapeDtypeStruct((64, 8, 128), F32)...]
where the time goes in v3:
time: 38.1 us; the launch traced here: 37.9 us
  Pallas kernels  34.9 us (92%)
  local copies, waits for them, and re-layouts  2.36 us (6%)
  between operations  0.65 us (2%)
    pallas_call x1, Pallas kernels, per_device(): pl.pallas_call(kernel, out_shape=(jax.ShapeDtypeStruct((64, 8, 128), F32)...  34.9 us
    unnamed x4, local copies, waits for them, and re-layouts  2.36 us

profile of v3, /device:TPU:1, one launch (start us, length us, event | category | flops | bytes accessed | tf_op | source)
XLA Modules:
  0.0 37.9 jit_solution(14346926311414558048)
XLA Ops:
  0.6 34.9 %shard_map.104 = (f32[64,8,128]{2,1,0:T(8,128)}, f32[32,8,128]{2,1,0:T(8,128)}) custom-call(f32[64,8,128]{2,1,0:T(8,128)} %cs_h.1, f32[3,64,8,128]{3,2,1,0:T(8,128)} %cv_h.1, f32[3,64,8,128]{3,2,1,0:T(8,128)} %cp_h.1, f32[32,8,128]{2,1,0:T(8,128)} %fs_h.1, f32[3,32,8,128]{3,2,1,0:T(8,128)} %fv_h.1, f32[3,32,8,128]{3,2,1,0:T(8,128)} %fp_h.1, ...), custom_call_target="tpu_custom_call" | custom-call | tf_op jit(solution)/shard_map/pallas_call | solution.py:756
  35.6 0.0 copy-start
  35.6 1.7 %copy.13 = f32[64,8,128]{2,1,0:T(8,128)} copy(f32[64,8,128]{2,1,0:T(8,128)} %get-tuple-element.4) | data formatting | bytes 524288
  37.3 0.0 copy-done
  37.3 0.7 %copy.14 = f32[32,8,128]{2,1,0:T(8,128)} copy(f32[32,8,128]{2,1,0:T(8,128)S(1)} %copy-done) | data formatting | bytes 262144
Async XLA Ops:
  35.6 1.7 %copy-start = (f32[32,8,128]{2,1,0:T(8,128)S(1)}, f32[32,8,128]{2,1,0:T(8,128)}, u32[]{:S(2)}) copy-start(f32[32,8,128]{2,1,0:T(8,128)} %get-tuple-element.5) | copy-start | bytes 393220

commit v4 on v3

--- a/solution.py
+++ b/solution.py
@@ -375,7 +375,7 @@
             pair(h, put)
             return carry
 
-        lax.fori_loop(at, end, step, 0, unroll=min(2, end - at))
+        lax.fori_loop(at, end, step, 0, unroll=end - at)
 
     def chunk_copy(k):
         at, end = chunks[k][0] // 2, chunks[k][1] // 2
@@ -505,7 +505,7 @@
                 wide[to + 4] = jnp.where(row < 4, pltpu.roll(rest, 6, 0), pltpu.roll(rest, 2, 0)) if e else rest
             return carry
 
-        lax.fori_loop(at // 2, end // 2, unpack, 0, unroll=min(2, (end - at) // 2))
+        lax.fori_loop(at // 2, end // 2, unpack, 0, unroll=(end - at) // 2)
         part, size = pl.ds(TILES * at, TILES * (end - at)), TILES * (end - at)
         res = split_dot(wide[part].reshape(size * 8, 128), zmat)
         for q in range(4):
@@ -543,7 +543,7 @@
             refine_plane(i, full)
             return carry
 
-        lax.fori_loop(at, end, step, 0)
+        lax.fori_loop(at, end, step, 0, unroll=2)
 
     def zup(t0, t1):
         a0, a1 = pltpu.roll(t0, 127, 1), pltpu.roll(t1, 127, 1)
@@ -623,11 +623,11 @@
 
     unpack_chunk(0)
     refine(3, 13, False)
-    carries = lax.fori_loop(1, 5, first_group, tuple(x_start(block, 6) for block in range(3)))
+    carries = lax.fori_loop(1, 5, first_group, tuple(x_start(block, 6) for block in range(3)), unroll=2)
     unpack_chunk(1)
     refine(13, 19, False)
     refine(19, 21, True)
-    lax.fori_loop(5, 9, first_group, carries)
+    lax.fori_loop(5, 9, first_group, carries, unroll=2)
     unpack_chunk(2)
     refine(1, 3, True)
     first_group(0, tuple(x_start(block, 2) for block in range(3)))

time: 38.1 us -> 37.2 us (0.976)
  Pallas kernels: 34.9 us -> 34 us
    pallas_call x1, Pallas kernels: 34.9 us -> 34 us  [per_device(): pl.pallas_call(kernel, out_shape=(jax.ShapeDtypeStruct((64, 8, 128), F32)...]
where the time goes in v4:
time: 37.2 us; the launch traced here: 37 us
  Pallas kernels  34 us (91%)
  local copies, waits for them, and re-layouts  2.36 us (6%)
  between operations  0.65 us (2%)
    pallas_call x1, Pallas kernels, per_device(): pl.pallas_call(kernel, out_shape=(jax.ShapeDtypeStruct((64, 8, 128), F32)...  34 us
    unnamed x4, local copies, waits for them, and re-layouts  2.36 us

profile of v4, /device:TPU:1, one launch (start us, length us, event | category | flops | bytes accessed | tf_op | source)
XLA Modules:
  0.0 37.0 jit_solution(292194079499266649)
XLA Ops:
  0.6 34.0 %shard_map.104 = (f32[64,8,128]{2,1,0:T(8,128)}, f32[32,8,128]{2,1,0:T(8,128)}) custom-call(f32[64,8,128]{2,1,0:T(8,128)} %cs_h.1, f32[3,64,8,128]{3,2,1,0:T(8,128)} %cv_h.1, f32[3,64,8,128]{3,2,1,0:T(8,128)} %cp_h.1, f32[32,8,128]{2,1,0:T(8,128)} %fs_h.1, f32[3,32,8,128]{3,2,1,0:T(8,128)} %fv_h.1, f32[3,32,8,128]{3,2,1,0:T(8,128)} %fp_h.1, ...), custom_call_target="tpu_custom_call" | custom-call | tf_op jit(solution)/shard_map/pallas_call | solution.py:756
  34.7 0.0 copy-start
  34.7 1.7 %copy.13 = f32[64,8,128]{2,1,0:T(8,128)} copy(f32[64,8,128]{2,1,0:T(8,128)} %get-tuple-element.4) | data formatting | bytes 524288
  36.4 0.0 copy-done
  36.4 0.7 %copy.14 = f32[32,8,128]{2,1,0:T(8,128)} copy(f32[32,8,128]{2,1,0:T(8,128)S(1)} %copy-done) | data formatting | bytes 262144
Async XLA Ops:
  34.7 1.7 %copy-start = (f32[32,8,128]{2,1,0:T(8,128)S(1)}, f32[32,8,128]{2,1,0:T(8,128)}, u32[]{:S(2)}) copy-start(f32[32,8,128]{2,1,0:T(8,128)} %get-tuple-element.5) | copy-start | bytes 393220
